TPU v7x, 32 devices: a whole 2x2x4 slice. The times are simulated.
32 devices in a mesh: gx: 8 (over y, x, core), gy: 4 (over z).
Axes of the slice: x: 2, y: 2, z: 4, core: 2. Of those that a mesh axis runs over, the one named last changes fastest.
Arguments:
- traces: bfloat16 [3, 48, 32, 16, 128], P(None, None, 'gx', 'gy'), may hold values from -6 to 6
- dirichlet: int32 [3, 32, 16, 128], P(None, 'gx', 'gy'), may hold values 0 or 1
- visc_class: int32 [32, 16, 128], P('gx', 'gy'), may hold values from 0 to 3
- viscosity: float32 [4], replicated, may hold values from 0.25 to 4
- coarse_diag: float32 [32, 16, 128], P('gx', 'gy'), may hold values from 2 to 16
- solve_map: bfloat16 [256, 288], replicated, may hold values from -0.375 to 0.375
- flux_map: bfloat16 [288, 256], replicated, may hold values from -0.375 to 0.375
Outputs:
- corrected: bfloat16 [3, 48, 32, 16, 128], P(None, None, 'gx', 'gy')
All inputs are finite; a program needn't handle non-finite values. No bound on the sum of `dirichlet` on one device may be relied on, other than what follows from the above.
Results may differ from a plain program's by a relative error of at most 0.005.
Values may be sent and summed in bfloat16 or wider, within the bound.
No kernel may reach another device: no remote copies, remote signals or barrier semaphores. Data moves between devices by JAX's collectives and lax.ppermute only.
A program may use at most 64 MiB of HBM per device.

v0:
```python
import functools
import math

import jax
import jax.numpy as jnp
import ml_dtypes
import numpy as np
from jax import lax
from jax.experimental import pallas as pl
from jax.experimental.pallas import tpu as pltpu
from jax.sharding import PartitionSpec as P

penalty = 0.5
BF = jnp.bfloat16
F32 = jnp.float32
lift = 1.3264
gain = 1.3280711361297461


def swap(value, axis, other, first, step=2):
    count, width = lax.axis_size(axis), lax.axis_size(other)
    place = (lambda i, j: i * width + j) if (axis, other) == ("gx", "gy") else (lambda i, j: j * count + i)
    lows = list(range(first, count - 1, step))
    pairs = [(place(low, j), place(low + 1, j)) for low in lows for j in range(width)]
    alone = [i for i in range(count) if i not in lows and i - 1 not in lows]
    pairs += [(place(i, j), place(i, j + 1)) for i in alone for j in range(0, width - 1, 2)]
    return lax.ppermute(value, ("gx", "gy"), pairs + [(high, low) for low, high in pairs])


def even(axis):
    return lax.rem(lax.axis_index(axis), 2) == 0


def arrive(messages, down_ref, up_ref):
    here, last = lax.axis_index("gy"), lax.axis_size("gy") - 1
    values = [ref[...] for ref in messages]
    for ref, swap_of, present in ((down_ref, lax.rem(here, 3), here < last), (up_ref, lax.rem(here + 2, 3), here > 0)):
        value = jnp.where(swap_of == 0, values[0], jnp.where(swap_of == 1, values[1], values[2]))
        ref[...] = jnp.where(present, value, jnp.zeros_like(value))


def depart_three(down_ref, up_ref, messages):
    here = lax.rem(lax.axis_index("gy"), 3)
    for k, ref in enumerate(messages):
        choose(here == k, up_ref, down_ref, ref)


def depart(axis, down_ref, up_ref, inner_ref, outer_ref):
    choose(even(axis), up_ref, down_ref, inner_ref)
    choose(even(axis), down_ref, up_ref, outer_ref)


def choose(condition, yes_ref, no_ref, out_ref, present=None):
    value = jnp.where(condition, yes_ref[...], no_ref[...])
    out_ref[...] = value if present is None else jnp.where(present, value, jnp.zeros_like(value))


def corner_table():
    gll_points = [-1.0, -math.sqrt(0.2), math.sqrt(0.2), 1.0]
    table = np.zeros((16, 4), np.float64)
    for s in range(4):
        for t in range(4):
            for p in range(2):
                for q in range(2):
                    table[4 * s + t, 2 * p + q] = (
                        (1 + (2 * p - 1) * gll_points[s]) * (1 + (2 * q - 1) * gll_points[t]) / 4
                    )
    return table


def landing(face_slot, high_s, high_t):
    direction, outward = divmod(face_slot, 2)
    if direction == 0:
        return (outward, high_s, high_t)
    if direction == 1:
        return (high_s, outward, high_t)
    return (high_s, high_t, outward)


def gather_table():
    weights = lift * corner_table()
    table = np.zeros((32, 288), np.float64)
    for slot in range(6):
        for s in range(2):
            for t in range(2):
                p, q, r = landing(slot, s, t)
                for c in range(3):
                    cols = slot * 48 + 16 * c + np.arange(16)
                    table[16 * r + 8 * p + 4 * q + c, cols] += weights[:, 2 * s + t]
    return table.astype(ml_dtypes.bfloat16)


def slot_table():
    slots = np.split(gather_table(), 6, axis=1)
    rows = [
        np.r_[0:8, 16:24], np.r_[8:16, 24:32], np.arange(32), np.arange(32), np.arange(16), np.arange(16, 32),
    ]
    return np.concatenate([slot[kept] for slot, kept in zip(slots, rows)], axis=0)


slot_rows = (0, 16, 32, 64, 96, 112, 128)


def between(low, high):
    step = high - low
    return [low, low + (0.5 - 0.5 * math.sqrt(0.2)) * step, low + (0.5 + 0.5 * math.sqrt(0.2)) * step, high]


def lanes(shape):
    return lax.broadcasted_iota(jnp.int32, shape, len(shape) - 1)


def z_next(value):
    last = value.shape[-1] - 1
    return jnp.where(lanes(value.shape) < last, pltpu.roll(value, last, value.ndim - 1), 0.0)


def z_prev(value):
    return jnp.where(lanes(value.shape) > 0, pltpu.roll(value, 1, value.ndim - 1), 0.0)


def dot(left, right):
    return jnp.dot(left, right, preferred_element_type=F32)


def wide(parts):
    return jnp.concatenate(parts, axis=1)


def tall(parts):
    return jnp.concatenate(parts, axis=0)


def columns(rows, count):
    z = rows.shape[1] // count
    return [rows[:, z * h : z * h + z] for h in range(count)]


def elements(slots):
    return tall([wide([hexa[s] for hexa in slots]) for s in range(6)])


def vertex_part(flux, parts_ref):
    rows = []
    for s in range(6):
        first, size = slot_rows[s], slot_rows[s + 1] - slot_rows[s]
        rows.append(dot(parts_ref[pl.ds(first, size), :], flux[48 * s : 48 * s + 48].astype(BF)))
    rows[2:4] = [rows[2] + rows[3]]
    return tall(rows)


def turned_dot(left, right):
    return lax.dot_general(left, right, (((1,), (1,)), ((), ())), preferred_element_type=F32)


def product(f_ref, st_ref, slot):
    first = 0 if slot is None else 48 * slot
    flux = turned_dot(f_ref[...], st_ref[...] if slot is None else st_ref[pl.ds(first, 48), :])
    rows = lax.broadcasted_iota(jnp.int32, flux.shape, 0)
    return flux, flux + jnp.where(rows == lax.broadcasted_iota(jnp.int32, flux.shape, 1) + first, F32(penalty), F32(0.0))


def slot_corners(traces, parts_ref, slot):
    z = traces[0].shape[1]
    first, size = slot_rows[slot], slot_rows[slot + 1] - slot_rows[slot]
    rows = dot(parts_ref[pl.ds(first, size), :], wide([trace.astype(BF) for trace in traces]))
    return [rows[:, z * h : z * h + z] for h in range(len(traces))]


def settle(rows, p):
    return rows[8 * p : 8 * p + 8] + z_prev(rows[16 + 8 * p : 24 + 8 * p])


def scaled_corners(delta, scales, offsets=(0, 1)):
    shape = (8, delta.shape[1])
    blank = jnp.zeros((1, shape[1]), F32)
    y_scale = jnp.where(
        lax.broadcasted_iota(jnp.int32, shape, 0) < 4,
        blank if scales[2] is None else scales[2], blank if scales[3] is None else scales[3],
    )
    results = []
    for p in offsets:
        parts = []
        for r in range(2):
            at = 32 + 16 * r + 8 * p
            part = delta[at : at + 8] * y_scale + delta[at + 32 : at + 40] * scales[4 + r]
            if scales[p] is not None:
                part = part + delta[16 * p + 8 * r : 16 * p + 8 * r + 8] * scales[p]
            parts.append(part)
        results.append(parts[0] + z_prev(parts[1]))
    return results


def level_visc(code, visc_ref):
    visc = jnp.zeros(code.shape, F32)
    for level in range(visc_ref.shape[0]):
        visc = visc + jnp.where(code == F32(level + 1), visc_ref[pl.ds(level, 1), :], F32(0.0))
    return visc


def merge(even, odd):
    odd = tall(odd)
    return tall(even) + pltpu.roll(odd, odd.shape[0] - 4, 0)


def first_kernel(
    wx, wy, visc_hbm, t_hbm, dir_hbm, cls_hbm, diag_hbm, st_hbm, f_hbm, parts_hbm,
    l_ref, nat, kp_ref, visc_ref, diag_ref, st_ref, f_ref, parts_ref, v_ref, v1_ref, v3_ref,
    swap0_ref, swap1_ref, swap2_ref, down_ref, up_ref, t_ref, dir_ref, cls_ref, levels, sems,
):
    cells = wx * wy
    pairs = [
        (parts_hbm, parts_ref), (f_hbm, f_ref), (st_hbm, st_ref), (t_hbm, t_ref), (dir_hbm, dir_ref),
        (cls_hbm, cls_ref), (visc_hbm, levels), (diag_hbm, diag_ref),
    ]
    copies = [pltpu.make_async_copy(a, b, sems.at[i]) for i, (a, b) in enumerate(pairs)]
    for copy in copies:
        copy.start()
    diagonal = lax.broadcasted_iota(jnp.int32, (288, 288), 0) == lax.broadcasted_iota(jnp.int32, (288, 288), 1)
    diagonal = jnp.where(diagonal, F32(penalty), F32(0.0))
    copies[0].wait()
    own = tall([vertex_part(diagonal, parts_ref), diagonal[144:192]])
    copies[1].wait()
    left = tall([vertex_part(f_ref[...], parts_ref).astype(BF), f_ref[pl.ds(144, 48), :]])
    for copy in copies[2:5]:
        copy.wait()
    short = (turned_dot(left, st_ref[...]) + own).astype(BF)
    z = t_ref.shape[2]
    for d in range(3):
        keep = (1 - dir_ref[d]).astype(F32)
        kp_ref[d] = keep
        masked = t_ref[d].astype(F32).reshape(48, cells, z) * keep[None]
        nat[d] = masked.reshape(48 * cells, z)
        lay_out(wx, wy, d, nat, l_ref, True)
    kp_ref[3] = z_next(kp_ref[2])
    for copy in copies[5:]:
        copy.wait()
    for level in range(visc_ref.shape[0]):
        visc_ref[pl.ds(level, 1), :] = jnp.full((1, z), levels[level], F32)
    code = cls_ref[...].astype(F32) + 1.0
    kp_ref[4] = level_visc(code, visc_ref)
    kp_ref[5] = code
    row = lambda i, col: kp_ref[i, pl.ds(col, 1), :]
    corners = []
    for side, y in enumerate((0, wy - 1)):
        where = [(x, y) for x in range(wx)]
        slots, scales, left_out = known_hexes(wx, wy, where, (l_ref, None), kp_ref)
        rows = columns(dot(short if side else short[0:96], elements(slots)), wx)
        corners += known_corners(rows, scales, left_out)
        v1_ref[side] = rows[wx - 1][16:32] * row(4, (wx - 1) * wy + y)
    place = lax.broadcasted_iota(jnp.int32, (32, z), 0)
    lone = [part * row(4, x * wy + wy - 1) for x, part in enumerate(rows)]
    for x in range(wx):
        v3_ref[x] = jnp.where(lax.rem(place, 8) < 4, 0.0, lone[x][32:64])
    sums = [line_sums(corners[:wx]), line_sums(corners[wx:])]
    for side in range(2):
        for i in range(wx + 1):
            v_ref[side, i] = sums[side][i]
    corner = (wx - 1) * wy
    top = wy - 1
    for x in range(wx):
        down_ref[pl.ds(48 * x, 48), :] = l_ref[1, x * wy]
        up_ref[pl.ds(48 * x, 48), :] = lone[x][96:144].astype(BF)
    down_ref[pl.ds(48 * wx, 48), :] = l_ref[0, 0]
    up_ref[pl.ds(48 * wx, 48), :] = l_ref[0, top]
    flags = [row(1, x * wy) for x in range(wx)] + [row(0, 0), row(5, corner), row(0, corner), row(2, corner)]
    diag = tall([diag_ref[pl.ds(x * wy, 1), :] for x in range(wx)])
    high = diag.astype(BF).astype(F32)
    rim = pack(sums[0], 0) + pack([v1_ref[0, 0:8], v1_ref[0, 8:16]], 0) + flags + [high, diag - high]
    put_tail(down_ref, 48 * wx + 48, rim)
    flags = [row(kind, x * wy + top) for kind in (5, 0, 2) for x in range(wx)]
    rim = pack(sums[1], 1) + pack([v1_ref[1, 0:8], v1_ref[1, 8:16]], 1) + flags
    put_tail(up_ref, 48 * wx + 48, rim)
    depart_three(down_ref, up_ref, (swap0_ref, swap1_ref, swap2_ref))


def tail_rows(count):
    return -(-count // 16) * 16


def put_tail(ref, start, rows):
    count = sum(part.shape[0] for part in rows)
    full = ref.shape[0] - start
    if full > count:
        rows = rows + [jnp.zeros((full - count, rows[0].shape[1]), F32)]
    ref[pl.ds(start, full), :] = tall(rows).astype(BF)


def pack(parts, half):
    place = lax.broadcasted_iota(jnp.int32, parts[0].shape, 0)
    parts = parts + [jnp.zeros_like(parts[0])] * (len(parts) % 2)
    packed = []
    for low, high in zip(parts[0::2], parts[1::2]):
        if half:
            low = pltpu.roll(low, 4, 0)
        else:
            high = pltpu.roll(high, 4, 0)
        packed.append(jnp.where(place < 4, low, high))
    return packed


def unpack(packed, count, half):
    parts = []
    for n in range(count):
        part = packed[8 * (n // 2) : 8 * (n // 2) + 8]
        parts.append(part if n % 2 == half else pltpu.roll(part, 4, 0))
    return parts


def read_tail(ref, wx, half):
    start = 48 * wx + 48
    rows = ref[pl.ds(start, ref.shape[0] - start), :].astype(F32)
    size = 8 * ((wx + 2) // 2)
    return unpack(rows, wx + 1, half), unpack(rows[size : size + 8], 2, half), rows[size + 8 :]


def line_sums(corners):
    low, high = [part[0] for part in corners], [part[1] for part in corners]
    return [low[0]] + [low[x] + high[x - 1] for x in range(1, len(low))] + [high[-1]]


def early(wx, wy, d, x, y):
    return y in (0, wy - 1) or (d == 0 and x == 0) or (d == 1 and y == 1)


def lay_out(wx, wy, d, nat, l_ref, first):
    for x in range(wx):
        for y in range(wy):
            if early(wx, wy, d, x, y) == first:
                col = x * wy + y
                part = nat[d, pl.ds(col, 48, stride=wx * wy), :]
                l_ref[d, col] = part.astype(BF)
                if d == 2:
                    l_ref[3, col] = z_next(part).astype(BF)


def known_hexes(wx, wy, where, l_refs, kp_ref):
    z = l_refs[0].shape[3]
    nothing = jnp.zeros((48, z), BF)
    row = lambda i, col: kp_ref[i, pl.ds(col, 1), :]
    trace = lambda d, x, y: l_refs[0 if early(wx, wy, min(d, 2), x, y) else 1][d, x * wy + y]
    slots, scales, left_out = [], [], []
    for x, y in where:
        here = x * wy + y
        visc = row(4, here)
        last_x, last_y = x == wx - 1, y == wy - 1
        slots.append(
            [
                trace(0, x, y), nothing if last_x else trace(0, x + 1, y),
                trace(1, x, y), nothing if last_y else trace(1, x, y + 1),
                trace(2, x, y), trace(3, x, y),
            ]
        )
        scales.append(
            [
                visc * row(0, here), visc if last_x else visc * row(0, here + wy),
                visc * row(1, here), visc if last_y else visc * row(1, here + 1),
                visc * row(2, here), visc * row(3, here),
            ]
        )
        left_out.append(([1] if last_x else []) + ([3] if last_y else []))
    return slots, scales, left_out


def known_corners(vertex, scales, left_out):
    return [
        scaled_corners(part, [None if s in out else scale[s] for s in range(6)])
        for part, scale, out in zip(vertex, scales, left_out)
    ]


def middle_kernel(
    wx, wy, l_ref, nat, kp_ref, st_ref, f_ref, parts_ref,
    c_ref, v_ref, v1_ref, mx_ref, my_ref, own_ref, rest_ref, m_ref, lost_ref,
):
    for slot, ref in ((1, mx_ref), (3, my_ref)):
        bare, flux = product(f_ref, st_ref, slot)
        turned = tall([bare[0:48], bare[96:288], bare[48:96]]) if slot == 1 else bare
        ref[pl.ds(0, 288), :] = turned.astype(BF)
        ref[pl.ds(288, 96), :] = vertex_part(flux, parts_ref).astype(BF)
    flux = product(f_ref, st_ref, None)[1]
    m_ref[pl.ds(0, 288), :] = flux.astype(BF)
    m_ref[pl.ds(288, 96), :] = vertex_part(flux, parts_ref).astype(BF)
    lost_ref[...] = (flux - flux.astype(BF).astype(F32))[:, 0:256].astype(BF)
    for d in range(3):
        lay_out(wx, wy, d, nat, rest_ref, False)
    own_ref[...] = dot(
        tall([my_ref[pl.ds(144, 48), :], my_ref[pl.ds(288, 96), :]]), wide([l_ref[1, x * wy] for x in range(wx)])
    )
    for y in range(wy):
        inside = 0 < y < wy - 1
        where = [(x, y) for x in range(wx)]
        slots, scales, left_out = known_hexes(wx, wy, where, (l_ref, rest_ref), kp_ref)
        element = elements(slots)
        rows = dot(m_ref[...] if inside else m_ref[pl.ds(0, 288), :], element)
        lost = columns(dot(lost_ref[...], element[0:256]), wx)
        rows = columns(rows, wx)
        for x in range(wx):
            for s in range(6):
                part = slice(48 * s, 48 * s + 48)
                c_ref[s, x * wy + y] = (rows[x][part] + lost[x][part]) * scales[x][s]
        if inside:
            corners = known_corners([part[288:] for part in rows], scales, left_out)
            v1_ref[y - 1] = rows[wx - 1][304:320] * kp_ref[4, pl.ds((wx - 1) * wy + y, 1), :]
            for i, part in enumerate(line_sums(corners)):
                v_ref[y - 1, i] = part


def after_y(wx, wy, xs, visc_ref, l_ref, kp_ref, parts_ref, my_ref, own_ref, v3_ref, down_ref, up_ref):
    z = l_ref.shape[3]
    misc_d = read_tail(down_ref, wx, 0)[2]
    misc_u = read_tail(up_ref, wx, 1)[2]
    row = lambda i, col: kp_ref[i, pl.ds(col, 1), :]
    delta = dot(my_ref[...], wide([down_ref[pl.ds(48 * x, 48), :] for x in xs]))
    arrived = [up_ref[pl.ds(48 * x, 48), :].astype(F32) for x in xs]
    arrived_corners = slot_corners(arrived, parts_ref, 3)
    results = []
    for n, x in enumerate(xs):
        here = x * wy + wy - 1
        last = x == wx - 1
        part = delta[:, z * n : z * n + z]
        visc = row(4, here)
        scales = [
            visc * row(0, here), visc if last else visc * row(0, here + wy), visc * row(1, here),
            visc * misc_d[x : x + 1], visc * row(2, here), visc * row(3, here),
        ]
        flux = [part[48 * s : 48 * s + 48] * scales[s] for s in range(6)]
        used = [None if (s == 1 and last) else scales[s] for s in range(6)]
        known = v3_ref[x] * misc_d[x : x + 1]
        top = [rows + settle(known, p) for p, rows in enumerate(scaled_corners(part[288:384], used))]
        top_one = part[304:320] * visc
        here = x * wy
        visc = level_visc(misc_u[x : x + 1], visc_ref)
        flag = row(1, here)
        own = own_ref[:, pl.ds(z * x, z)]
        keep_z = misc_u[2 * wx + x : 2 * wx + x + 1]
        scales = [
            visc * misc_u[wx + x : wx + x + 1], None if last else visc * misc_u[wx + x + 1 : wx + x + 2],
            None, visc * flag, visc * keep_z, visc * z_next(keep_z),
        ]
        known = arrived_corners[n] * flag
        low = [rows + settle(known, p) for p, rows in enumerate(scaled_corners(own[48:144], scales))]
        low_one = own[64:80] * visc
        face = (arrived[n] + visc * (own[0:48] + penalty * l_ref[1, here].astype(F32))) * flag
        results.append((flux, top, top_one, low, low_one, face))
    return results


def turn_kernel(
    wx, wy, visc_ref, l_ref, kp_ref, diag_ref, parts_ref, my_ref, own_ref, c_ref, va_ref, vb_ref,
    v1a_ref, v1b_ref, v3_ref, swap0_in, swap1_in, swap2_in,
    c3_ref, vt_ref, vl_ref, v1_ref, face_ref, yd_ref, yu_ref, inner_ref, outer_ref, down_ref, up_ref,
):
    z = l_ref.shape[3]
    arrive((swap0_in, swap1_in, swap2_in), yd_ref, yu_ref)
    xs = (0, wx - 1)
    results = after_y(wx, wy, xs, visc_ref, l_ref, kp_ref, parts_ref, my_ref, own_ref, v3_ref, yd_ref, yu_ref)
    row = lambda i, col: kp_ref[i, pl.ds(col, 1), :]
    sums_d, one_d, misc_d = read_tail(yd_ref, wx, 0)
    sums_u, one_u, misc_u = read_tail(yu_ref, wx, 1)
    edge_high, edge_low = misc_d[wx + 4 : 2 * wx + 4], misc_d[2 * wx + 4 : 3 * wx + 4]
    for n, (flux, top, top_one, low, low_one, face) in enumerate(results):
        for s in range(6):
            c3_ref[n, s] = flux[s]
        face_ref[n] = face
        for p in range(2):
            vt_ref[n, p] = top[p]
            vl_ref[n, p] = low[p]
    flux, top, top_one, low, low_one, face = results[1]
    mine = tall(one_u) + low_one
    v1_ref[0] = mine
    v1_ref[1] = v1a_ref[0]
    for y in range(wy - 2):
        v1_ref[2 + y] = v1b_ref[y]
    v1_ref[wy] = v1a_ref[1] + top_one
    v1_ref[wy + 1] = tall(one_d)

    def plane(i, n, p):
        lines = [sums_u[i] + vl_ref[n, p], va_ref[0, i]]
        lines += [vb_ref[y, i] for y in range(wy - 2)]
        lines += [va_ref[1, i] + vt_ref[n, p], sums_d[i]]
        return merge(lines[1::2], lines[0::2])

    down_ref[pl.ds(0, 48), :] = yu_ref[pl.ds(48 * wx, 48), :]
    for y in range(wy):
        down_ref[pl.ds(48 + 48 * y, 48), :] = l_ref[0, y]
    down_ref[pl.ds(48 * (wy + 1), 48), :] = yd_ref[pl.ds(48 * wx, 48), :]
    diag = diag_ref[pl.ds(0, wy), :]
    high = diag.astype(BF).astype(F32)
    rim = [plane(0, 0, 0), high, edge_high[0:1], diag - high, edge_low[0:1]]
    rim += [misc_u[wx : wx + 1], kp_ref[0, 0:wy], misc_d[wx : wx + 1]]
    put_tail(down_ref, 48 * (wy + 2), rim)
    corner = (wx - 1) * wy
    for y in range(wy):
        part = c_ref[1, corner + y]
        up_ref[pl.ds(48 * y, 48), :] = (part + flux[1] if y == wy - 1 else part).astype(BF)
    last = pl.ds(corner, wy)
    rim = [plane(wx, 1, 1), mine, *one_d]
    rim += [misc_u[wx - 1 : wx], kp_ref[5, last], misc_d[wx + 1 : wx + 2]]
    rim += [misc_u[3 * wx - 1 : 3 * wx], kp_ref[2, last], misc_d[wx + 3 : wx + 4]]
    rim += [kp_ref[1, last], misc_d[wx - 1 : wx]]
    put_tail(up_ref, 48 * wy, rim)
    depart("gx", down_ref, up_ref, inner_ref, outer_ref)


def assemble_kernel(
    wx, wy, visc_ref, l_ref, kp_ref, diag_ref, parts_ref, mx_ref, my_ref, own_ref, c_ref, c3_ref,
    va_ref, vb_ref, v3_ref, vt_ref, vl_ref, face_ref, yd_ref, yu_ref,
    r_ref, late_ref, v_ref, inv_ref, ownx_ref, mid,
):
    z = l_ref.shape[3]
    cells = wx * wy
    xs = tuple(range(1, wx - 1))
    results = after_y(wx, wy, xs, visc_ref, l_ref, kp_ref, parts_ref, my_ref, own_ref, v3_ref, yd_ref, yu_ref)
    for n, part in enumerate(results):
        for s in range(6):
            mid[n, s] = part[0][s]
    traces = [yu_ref[pl.ds(48 * wx, 48), :]] + [l_ref[0, y] for y in range(wy)] + [yd_ref[pl.ds(48 * wx, 48), :]]
    ownx_ref[...] = dot(mx_ref[pl.ds(240, 144), :], wide(traces))

    def contrib(slot, x, y):
        here = c_ref[slot, x * wy + y]
        if y < wy - 1:
            return here
        return here + (mid[x - 1, slot] if 0 < x < wx - 1 else c3_ref[0 if x == 0 else 1, slot])

    for x in range(wx):
        for y in range(wy):
            col = pl.ds(x * wy + y, 48, stride=cells)
            if y:
                behind = contrib(3, x, y - 1)
            elif 0 < x < wx - 1:
                behind = results[x - 1][5]
            else:
                behind = face_ref[0 if x == 0 else 1]
            ahead = contrib(0, x, y) + contrib(1, x - 1, y) if x else contrib(0, x, y)
            sides = [ahead, contrib(2, x, y) + behind, contrib(4, x, y) + z_prev(contrib(5, x, y))]
            for d in range(3):
                if x == wx - 1:
                    late_ref[d, y] = sides[d]
                elif d == 0 and x == 0:
                    late_ref[3, y] = sides[d]
                else:
                    r_ref[d, col, :] = sides[d]
    sums_d, one_d, misc_d = read_tail(yd_ref, wx, 0)
    sums_u, one_u, misc_u = read_tail(yu_ref, wx, 1)
    edge_diag = misc_d[wx + 4 : 2 * wx + 4] + misc_d[2 * wx + 4 : 3 * wx + 4]

    def brought(which, i):
        held = vt_ref if which == 1 else vl_ref
        terms = []
        for x, p in ((i, 0), (i - 1, 1)):
            if x in (0, wx - 1):
                terms.append(held[0 if x == 0 else 1, p])
            elif 0 < x < wx - 1:
                terms.append(results[x - 1][which][p])
        return sum(terms[1:], terms[0])

    for i in range(wx + 1):
        lines = [sums_u[i] + brought(3, i), va_ref[0, i]]
        lines += [vb_ref[y, i] for y in range(wy - 2)]
        lines += [va_ref[1, i] + brought(1, i), sums_d[i]]
        v_ref[i] = merge(lines[1::2], lines[0::2])
        if i < wx:
            parts = [jnp.broadcast_to(diag_ref[pl.ds(i * wy + y, 1), :], (4, z)) for y in range(wy)]
            parts += [jnp.broadcast_to(edge_diag[i : i + 1], (4, z)), jnp.zeros((4, z), F32)]
            inv_ref[i] = reciprocal(tall(parts))


def reciprocal(diag):
    present = diag > 0.0
    return jnp.where(present, (1.0 / gain) / jnp.where(present, diag, 1.0), 0.0)


def final_kernel(
    wx, wy, visc_ref, l_ref, kp_ref, parts_ref, mx_ref, ownx_ref, r_in, late_ref, v_ref, inv_ref, v1_ref,
    yd_ref, yu_ref, outer_in, inner_in, out_hbm, r_ref, held, fix, sems,
):
    here, last = lax.axis_index("gx"), lax.axis_size("gx") - 1

    def from_high(start, size):
        rows = pl.ds(start, size)
        value = jnp.where(even("gx"), inner_in[rows, :], outer_in[rows, :])
        return jnp.where(here < last, value, jnp.zeros_like(value))

    def from_low(start, size):
        rows = pl.ds(start, size)
        value = jnp.where(even("gx"), outer_in[rows, :], inner_in[rows, :])
        return jnp.where(here > 0, value, jnp.zeros_like(value))

    cells, z = wx * wy, l_ref.shape[3]
    rows = v_ref.shape[1]
    row = lambda i, col: kp_ref[i, pl.ds(col, 1), :]
    traces = [from_high(48 * j, 48) for j in range(wy + 2)]
    delta = dot(mx_ref[pl.ds(288, 96), :], wide(traces))
    rim_x = from_high(48 * (wy + 2), tail_rows(rows + 3 * wy + 4)).astype(F32)
    rim_l = from_low(48 * wy, tail_rows(rows + 32 + 3 * (wy + 2) - 1)).astype(F32)
    misc_d = read_tail(yd_ref, wx, 0)[2]
    misc_u = read_tail(yu_ref, wx, 1)[2]
    flags_high = rim_x[rows + 2 * (wy + 1) : rows + 3 * wy + 4]
    corner = (wx - 1) * wy
    arrived = [from_low(48 * y, 48) for y in range(wy)]
    arrived_corners = slot_corners(arrived, parts_ref, 1)
    codes = rim_l[rows + 32 : rows + 32 + wy + 2]
    keep_z = rim_l[rows + 32 + wy + 2 : rows + 32 + 2 * (wy + 2)]
    keep_y = rim_l[rows + 32 + 2 * (wy + 2) : rows + 32 + 3 * (wy + 2) - 1]
    low_visc = level_visc(codes, visc_ref)
    low_keep_z = z_next(keep_z)
    lines = [[], [], []]
    high_scales = []
    del r_in
    for j in range(-1, wy + 1):
        n = j + 1
        part = delta[:, z * n : z * n + z]
        flag = flags_high[n : n + 1]
        if j < 0:
            visc = level_visc(misc_u[wx - 1 : wx], visc_ref)
            kz = misc_u[3 * wx - 1 : 3 * wx]
            keeps = [misc_u[2 * wx - 1 : 2 * wx], flag, None, row(1, corner), kz, z_next(kz)]
        elif j < wy:
            here = corner + j
            visc = row(4, here)
            high_y = row(1, here + 1) if j < wy - 1 else misc_d[wx - 1 : wx]
            keeps = [row(0, here), flag, row(1, here), high_y, row(2, here), row(3, here)]
        else:
            visc = level_visc(misc_d[wx + 1 : wx + 2], visc_ref)
            kz = misc_d[wx + 3 : wx + 4]
            keeps = [misc_d[wx + 2 : wx + 3], flag, misc_d[wx - 1 : wx], None, kz, z_next(kz)]
        scales = [None if keep is None else visc * keep for keep in keeps]
        corners = scaled_corners(part, scales)
        one = v1_ref[n] * flag
        lines[0].append(corners[0])
        lines[1].append(corners[1] + one[0:8] + z_prev(one[8:16]))
        high_scales.append(scales)
        own = ownx_ref[:, pl.ds(z * n, z)]
        visc = low_visc[n : n + 1]
        flag = misc_u[wx : wx + 1] if j < 0 else misc_d[wx : wx + 1] if j == wy else row(0, j)
        scales = [
            None, visc * flag, None if j < 0 else visc * keep_y[j : j + 1],
            None if j == wy else visc * keep_y[j + 1 : j + 2], visc * keep_z[n : n + 1], visc * low_keep_z[n : n + 1],
        ]
        corners = scaled_corners(own[48:144], scales, (1,))[0]
        if 0 <= j < wy:
            one = arrived_corners[j] * flag
            lines[2].append(corners + one[0:8] + z_prev(one[8:16]))
            face = (arrived[j].astype(F32) + visc * (own[0:48] + penalty * l_ref[0, j].astype(F32))) * flag
            r_ref[0, pl.ds(j, 48, stride=cells), :] = late_ref[3, j] + face
        else:
            at = rows + (0 if j < 0 else 16)
            one = rim_l[at : at + 16] * flag
            lines[2].append(corners + one[0:8] + z_prev(one[8:16]))
    low, before, first = [merge(part[1::2], part[0::2]) for part in lines]
    top = v_ref[wx] + before + rim_x[0:rows]
    values = [(v_ref[0] + first + rim_l[0:rows]) * inv_ref[0]]
    values += [v_ref[i] * inv_ref[i] for i in range(1, wx - 1)]
    values += [(v_ref[wx - 1] + low) * inv_ref[wx - 1]]
    diag = rim_x[rows : rows + wy + 1] + rim_x[rows + wy + 1 : rows + 2 * (wy + 1)]
    parts = [jnp.broadcast_to(diag[j : j + 1], (4, z)) for j in range(wy + 1)]
    values += [top * reciprocal(tall(parts + [jnp.zeros((rows - 4 * (wy + 1), z), F32)]))]
    high = [pltpu.roll(value, rows - 4, 0) for value in values]
    for i in range(wx + 1):
        fix[0, pl.ds(4 * wy * i, 4 * wy), :] = values[i][0 : 4 * wy]
        fix[1, pl.ds(4 * wy * i, 4 * wy), :] = high[i][0 : 4 * wy]
    vertex = lambda c, p, q: fix[q, pl.ds(4 * wy * p + c, cells, stride=4), :]
    delta = columns(dot(mx_ref[pl.ds(0, 240), :], wide(traces[1 : wy + 1])), wy)
    behind = dot(mx_ref[pl.ds(96, 48), :], traces[0]) * high_scales[0][3]
    copies = []
    for d in range(3):
        for j in range(wy):
            scales = high_scales[j + 1]
            part = [delta[j][48 * i : 48 * i + 48] for i in range(5)]
            if d == 0:
                flux = part[0] * scales[0]
            elif d == 1:
                flux = part[1] * scales[2] + behind
                behind = part[2] * scales[3]
            else:
                flux = part[3] * scales[4] + z_prev(part[4] * scales[5])
            r_ref[d, pl.ds(corner + j, 48, stride=cells), :] = late_ref[d, j] + flux
        flags = kp_ref[d]
        for c in range(3):
            if d == 0:
                near = [vertex(c, 0, q) * flags for q in range(2)]
                far = [z_next(vertex(c, 0, q)) * flags for q in range(2)]
                corner_values = [[near[0], far[0]], [near[1], far[1]]]
            elif d == 1:
                corner_values = [[vertex(c, p, 0) * flags, z_next(vertex(c, p, 0)) * flags] for p in range(2)]
            else:
                corner_values = [[vertex(c, p, q) * flags for q in range(2)] for p in range(2)]
            lines = [between(corner_values[0][t], corner_values[1][t]) for t in range(2)]
            for a in range(4):
                for b, value in enumerate(between(lines[0][a], lines[1][a])):
                    at = pl.ds(cells * (16 * c + 4 * a + b), cells)
                    held[d, at, :] = (r_ref[d, at, :] + value).astype(BF)
            part = pl.ds(16 * cells * c, 16 * cells)
            copies.append(pltpu.make_async_copy(held.at[d, part], out_hbm.at[d, part], sems.at[3 * d + c]))
            copies[-1].start()
    for copy in copies:
        copy.wait()


def call(body, args, outs, scratch, flops, hbm=False, aliases=None):
    if hbm:
        args = tuple(pltpu.with_memory_space_constraint(a, pltpu.HBM) for a in args)
    keywords = {}
    if aliases:
        spaces = [pltpu.HBM] + [pltpu.VMEM] * (len(outs) - 1)
        keywords = dict(out_specs=tuple(pl.BlockSpec(memory_space=space) for space in spaces), input_output_aliases=aliases)
    return pl.pallas_call(
        body,
        **keywords,
        in_specs=[pl.BlockSpec(memory_space=pltpu.HBM if hbm else pltpu.VMEM)] * len(args),
        out_shape=outs,
        scratch_shapes=scratch,
        cost_estimate=pl.CostEstimate(flops=flops, bytes_accessed=1000000, transcendentals=0),
        compiler_params=pltpu.CompilerParams(vmem_limit_bytes=16 * 1024 * 1024),
    )(*args)


def local(traces, dirichlet, visc_class, viscosity, coarse_diag, solve_map, flux_map):
    wx, wy, z = traces.shape[2:]
    cells = wx * wy
    rows = 8 * (wy // 2 + 1)
    per_hex = 2 * 384 * 288 * z
    parts = jnp.asarray(slot_table())
    vm = pltpu.VMEM
    bind = lambda body: functools.partial(body, wx, wy)
    y_message = vm((48 * wx + 48 + tail_rows(8 * ((wx + 2) // 2) + 8 + 3 * wx + 4), z), BF)
    x_message = vm((48 * (wy + 2) + tail_rows(rows + 3 * wy + 4), z), BF)

    (lifted, nat, flags, visc, diag, s_turned, f_map, parts, va, v1a, v3, *swaps) = call(
        bind(first_kernel),
        (
            viscosity, traces.reshape(3, 48 * cells, z), dirichlet.reshape(3, cells, z),
            visc_class.reshape(cells, z), coarse_diag.reshape(cells, z), solve_map.T, flux_map, parts,
        ),
        (
            vm((4, cells, 48, z), BF), vm((3, 48 * cells, z), F32), vm((6, cells, z), F32), vm((viscosity.shape[0], z), F32), vm((cells, z), F32),
            vm(solve_map.shape[::-1], BF), vm(flux_map.shape, BF), vm(parts.shape, BF),
            vm((2, wx + 1, 8, z), F32), vm((2, 16, z), F32), vm((wx, 32, z), F32),
            y_message, y_message, y_message,
        ),
        [
            y_message, y_message,
            vm((3, 48 * cells, z), BF), vm((3, cells, z), jnp.int32), vm((cells, z), jnp.int32),
            pltpu.SMEM(viscosity.shape, F32), pltpu.SemaphoreType.DMA((8,)),
        ],
        wx * per_hex, True,
    )
    swaps = [swap(message, "gy", "gx", k, 3) for k, message in enumerate(swaps)]
    c, vb, v1b, mx, my, own = call(
        bind(middle_kernel),
        (lifted, nat, flags, s_turned, f_map, parts),
        (
            vm((6, cells, 48, z), F32), vm((wy - 2, wx + 1, 8, z), F32), vm((wy - 2, 16, z), F32),
            vm((384, 48), BF), vm((384, 48), BF), vm((144, wx * z), F32),
        ),
        [vm((4, cells, 48, z), BF), vm((384, 288), BF), vm((288, 256), BF)], cells * per_hex,
    )
    c3, vt, vl, v1, face, yd, yu, inner, outer = call(
        bind(turn_kernel),
        (
            visc, lifted, flags, diag, parts, my, own, c, va, vb, v1a, v1b, v3, *swaps,
        ),
        (
            vm((2, 6, 48, z), F32), vm((2, 2, 8, z), F32), vm((2, 2, 8, z), F32), vm((wy + 2, 16, z), F32),
            vm((2, 48, z), F32), y_message, y_message, x_message, x_message,
        ),
        [x_message, x_message], 2 * per_hex,
    )
    inner = swap(inner, "gx", "gy", 0)
    outer = swap(outer, "gx", "gy", 1)
    residual, late, vs, inverse, ownx = call(
        bind(assemble_kernel),
        (
            visc, lifted, flags, diag, parts, mx, my, own, c, c3, va, vb, v3, vt, vl, face, yd, yu,
        ),
        (
            vm((3, 48 * cells, z), F32), vm((4, wy, 48, z), F32), vm((wx + 1, rows, z), F32), vm((wx, rows, z), F32),
            vm((144, (wy + 2) * z), F32),
        ),
        [vm((wx - 2, 6, 48, z), F32)], 4 * per_hex,
    )
    out, _ = call(
        bind(final_kernel),
        (
            visc, lifted, flags, parts, mx, ownx, residual, late, vs, inverse, v1, yd, yu, outer, inner,
        ),
        (jax.ShapeDtypeStruct((3, 48 * cells, z), BF), vm((3, 48 * cells, z), F32)),
        [vm((3, 48 * cells, z), BF), vm((2, 4 * wy * (wx + 1), z), F32), pltpu.SemaphoreType.DMA((9,))], 6 * per_hex,
        aliases={6: 1},
    )
    return out.reshape(traces.shape)


def solution(mesh):
    in_specs = (
        P(None, None, "gx", "gy", None),
        P(None, "gx", "gy", None),
        P("gx", "gy", None),
        P(),
        P("gx", "gy", None),
        P(),
        P(),
    )
    out_specs = P(None, None, "gx", "gy", None)
    return jax.shard_map(local, mesh=mesh, in_specs=in_specs, out_specs=out_specs, check_vma=False)
```

profile of v0, /device:TPU:0, one launch (start us, length us, event | category | flops | bytes accessed | tf_op | source)
XLA Modules:
  0.0 14.1 jit_solution(13764631332502213429)
XLA Ops:
  0.0 2.2 %shard_map.82 = (bf16[4,16,48,128]{3,2,1,0:T(8,128)(2,1)S(1)}, f32[3,768,128]{2,1,0:T(8,128)S(1)}, f32[6,16,128]{2,1,0:T(8,128)S(1)}, f32[4,128]{1,0:T(4,128)S(1...) custom-call(f32[4]{0:T(128)} %visc_hbm.1, ...), custom_call_target="tpu_custom_call" | custom-call | flops 113246208 | bytes 1000000 | tf_op jit(solution)/shard_map/pallas_call | solution.py:709
  2.2 3.1 %collective-permute-start = (bf16[288,128]{1,0:T(8,128)(2,1)S(1)}, bf16[288,128]{1,0:T(8,128)(2,1)S(1)}, u32[]{:S(2)}, u32[]{:S(2)}) collective-permute-start(bf16[288,128]{1,0:T(8,128)(2,1)S(1)} %get-tuple-element.57), channel_id=1, source_target_pairs={{0,1},{4,5},{8,9},{12,13},{16,17},{20,21},{24,25},{28,29},{2,6},{1... | collective-permute-start | bytes 221192 | tf_op jit(solution)/shard_map/ppermute | solution.py:27
  5.3 0.0 collective-permute-start.1
  5.3 0.5 %collective-permute-start.2 = (bf16[288,128]{1,0:T(8,128)(2,1)S(1)}, bf16[288,128]{1,0:T(8,128)(2,1)S(1)}, u32[]{:S(2)}, u32[]{:S(2)}) collective-permute-start(bf16[288,128]{1,0:T(8,128)(2,1)S(1)} %get-tuple-element.59), channel_id=1, source_target_pairs={{2,3},{6,7},{10,11},{14,15},{18,19},{22,23},{26,27},{30,31},{0,4},... | collective-permute-start | bytes 221192 | tf_op jit(solution)/shard_map/ppermute | solution.py:27
  5.8 1.9 %shard_map.83 = (f32[6,16,48,128]{3,2,1,0:T(8,128)S(1)}, f32[2,5,8,128]{3,2,1,0:T(8,128)S(1)}, f32[2,16,128]{2,1,0:T(8,128)S(1)}, bf16[384,48]{1,0:T(8,128)(2,1)...) custom-call(bf16[4,16,48,128]{3,2,1,0:T(8,128)(2,1)S(1)} %get-tuple-element.41.l_ref, ...), custom_call_target="tpu_custom_call" | custom-call | flops 452984832 | bytes 1000000 | tf_op jit(solution)/shard_map/pallas_call | solution.py:709
  7.6 0.0 collective-permute-done.swap0_in
  7.7 0.0 collective-permute-done.1.swap1_in
  7.7 0.0 collective-permute-done.2.swap2_in
  7.7 0.3 %shard_map.84 = (f32[2,6,48,128]{3,2,1,0:T(8,128)S(1)}, f32[2,2,8,128]{3,2,1,0:T(8,128)S(1)}, f32[2,2,8,128]{3,2,1,0:T(8,128)S(1)}, f32[6,16,128]{2,1,0:T(8,128)...) custom-call(f32[4,128]{1,0:T(4,128)S(1)} %get-tuple-element.40.visc_, ...), custom_call_target="tpu_custom_call" | custom-call | flops 56623104 | bytes 1000000 | tf_op jit(solution)/shard_map/pallas_call | solution.py:709
  8.0 2.2 %collective-permute-start.3 = (bf16[336,128]{1,0:T(8,128)(2,1)S(1)}, bf16[336,128]{1,0:T(8,128)(2,1)S(1)}, u32[]{:S(2)}, u32[]{:S(2)}) collective-permute-start(bf16[336,128]{1,0:T(8,128)(2,1)S(1)} %get-tuple-element.72), channel_id=1, source_target_pairs={{4,8},{5,9},{6,10},{7,11},{12,16},{13,17},{14,18},{15,19},{20,24},... | collective-permute-start | bytes 258056 | tf_op jit(solution)/shard_map/ppermute | solution.py:27
  10.2 0.0 collective-permute-start.4
  10.2 0.5 %shard_map.85 = (f32[3,768,128]{2,1,0:T(8,128)S(1)}, f32[4,4,48,128]{3,2,1,0:T(8,128)S(1)}, f32[5,24,128]{2,1,0:T(8,128)S(1)}, f32[4,24,128]{2,1,0:T(8,128)S(1)}, f32[144,768]{1,0:T(8,128)S(1)}) custom-call(f32[4,128]{1,0:T(4,128)S(1)} %get-tuple-element.40.visc_ref, bf16[4,16,48,128]{3,2,1,0:T(8,128)(2,1)S(1)} %get-tuple-element.41.l_ref, ...), custom_call_target="tpu_custom_call" | custom-call | flops 113246208 | bytes 1000000 | tf_op jit(solution)/shard_map/pallas_call | solution.py:709
  10.7 1.9 %collective-permute-done.3.outer_in = bf16[336,128]{1,0:T(8,128)(2,1)S(1)} collective-permute-done((bf16[336,128]{1,0:T(8,128)(2,1)S(1)}, bf16[336,128]{1,0:T(8,128)(2,1)S(1)}, u32[]{:S(2)}, u32[]{:S(2)}) %collective-permute-start.3) | collective-permute-done | bytes 86048 | tf_op jit(solution)/shard_map/ppermute | solution.py:27
  12.6 0.0 collective-permute-done.4.inner_in
  12.6 1.4 %shard_map.86 = (bf16[3,768,128]{2,1,0:T(8,128)(2,1)}, f32[3,768,128]{2,1,0:T(8,128)S(1)}) custom-call(f32[4,128]{1,0:T(4,128)S(1)} %get-tuple-element.40.visc_ref, bf16[4,16,48,128]{3,2,1,0:T(8,128)(2,1)S(1)} %get-tuple-element.41.l_ref, f32[6,16,128]{2,1,0:T(8,128)S(1)} %get-tuple-element.42.kp_ref, ...), custom_call_target="tpu_custom_call", output_to_operand_aliasing={{1}: (6, {})} | custom-call | flops 169869312 | bytes 1000000 | tf_op jit(solution)/shard_map/pallas_call | solution.py:709
Async XLA Ops:
  2.2 5.5 %collective-permute-start = (bf16[288,128]{1,0:T(8,128)(2,1)S(1)}, bf16[288,128]{1,0:T(8,128)(2,1)S(1)}, u32[]{:S(2)}, u32[]{:S(2)}) collective-permute-start(bf16[288,128]{1,0:T(8,128)(2,1)S(1)} %get-tuple-element.57), channel_id=1, source_target_pairs={{0,1},{4,5},{8,9},{12,13},{16,17},{20,21},{24,25},{28,29},{2,6},{1... | collective-permute-start | bytes 221192 | tf_op jit(solution)/shard_map/ppermute | solution.py:27
  5.3 2.4 %collective-permute-start.1 = (bf16[288,128]{1,0:T(8,128)(2,1)S(1)}, bf16[288,128]{1,0:T(8,128)(2,1)S(1)}, u32[]{:S(2)}, u32[]{:S(2)}) collective-permute-start(bf16[288,128]{1,0:T(8,128)(2,1)S(1)} %get-tuple-element.58), channel_id=1, source_target_pairs={{1,2},{5,6},{9,10},{13,14},{17,18},{21,22},{25,26},{29,30},{0,4},{... | collective-permute-start | bytes 221192 | tf_op jit(solution)/shard_map/ppermute | solution.py:27
  5.3 2.4 %collective-permute-start.2 = (bf16[288,128]{1,0:T(8,128)(2,1)S(1)}, bf16[288,128]{1,0:T(8,128)(2,1)S(1)}, u32[]{:S(2)}, u32[]{:S(2)}) collective-permute-start(bf16[288,128]{1,0:T(8,128)(2,1)S(1)} %get-tuple-element.59), channel_id=1, source_target_pairs={{2,3},{6,7},{10,11},{14,15},{18,19},{22,23},{26,27},{30,31},{0,4},... | collective-permute-start | bytes 221192 | tf_op jit(solution)/shard_map/ppermute | solution.py:27
  8.0 4.6 %collective-permute-start.3 = (bf16[336,128]{1,0:T(8,128)(2,1)S(1)}, bf16[336,128]{1,0:T(8,128)(2,1)S(1)}, u32[]{:S(2)}, u32[]{:S(2)}) collective-permute-start(bf16[336,128]{1,0:T(8,128)(2,1)S(1)} %get-tuple-element.72), channel_id=1, source_target_pairs={{4,8},{5,9},{6,10},{7,11},{12,16},{13,17},{14,18},{15,19},{20,24},... | collective-permute-start | bytes 258056 | tf_op jit(solution)/shard_map/ppermute | solution.py:27
  10.2 2.5 %collective-permute-start.4 = (bf16[336,128]{1,0:T(8,128)(2,1)S(1)}, bf16[336,128]{1,0:T(8,128)(2,1)S(1)}, u32[]{:S(2)}, u32[]{:S(2)}) collective-permute-start(bf16[336,128]{1,0:T(8,128)(2,1)S(1)} %get-tuple-element.73), channel_id=1, source_target_pairs={{0,4},{1,5},{2,6},{3,7},{8,12},{9,13},{10,14},{11,15},{16,20},{17,... | collective-permute-start | bytes 258056 | tf_op jit(solution)/shard_map/ppermute | solution.py:27
where the time goes:
time: 14.3 us; the launch traced here: 14.1 us
  Pallas kernels  6.34 us (44%)
  starting transfers between devices  5.74 us (40%)
  waiting for transfers between devices  1.92 us (13%)
    pallas_call x5, Pallas kernels, call(): pl.pallas_call(body, **keywords, in_specs=[pl.BlockSpec(memory_space=pltp...  6.34 us
    ppermute x5, starting transfers between devices, swap(): lax.ppermute(value, ('gx', 'gy'), pairs + [(high, low) for low, high in p...  5.74 us
    ppermute x5, waiting for transfers between devices, swap(): lax.ppermute(value, ('gx', 'gy'), pairs + [(high, low) for low, high in p...  1.92 us
  transfers between devices with their start and end apart: 5, of which 1 were waited for; matrix products, arithmetic and copies ran while one was open for 0% of the time, Pallas kernels for 17%

commit v1 on v0

--- a/solution.py
+++ b/solution.py
@@ -210,9 +210,11 @@
 ):
     cells = wx * wy
     pairs = [
-        (parts_hbm, parts_ref), (f_hbm, f_ref), (st_hbm, st_ref), (t_hbm, t_ref), (dir_hbm, dir_ref),
+        (parts_hbm, parts_ref), (f_hbm, f_ref), (st_hbm, st_ref), (dir_hbm, dir_ref),
         (cls_hbm, cls_ref), (visc_hbm, levels), (diag_hbm, diag_ref),
     ]
+    half = pl.ds(0, 24 * cells), pl.ds(24 * cells, 24 * cells)
+    pairs[3:3] = [(t_hbm.at[d, part], t_ref.at[d, part]) for d in range(3) for part in half]
     copies = [pltpu.make_async_copy(a, b, sems.at[i]) for i, (a, b) in enumerate(pairs)]
     for copy in copies:
         copy.start()
@@ -222,7 +224,7 @@
     own = tall([vertex_part(diagonal, parts_ref), diagonal[144:192]])
     copies[1].wait()
     left = tall([vertex_part(f_ref[...], parts_ref).astype(BF), f_ref[pl.ds(144, 48), :]])
-    for copy in copies[2:5]:
+    for copy in copies[2:10]:
         copy.wait()
     short = (turned_dot(left, st_ref[...]) + own).astype(BF)
     z = t_ref.shape[2]
@@ -233,7 +235,7 @@
         nat[d] = masked.reshape(48 * cells, z)
         lay_out(wx, wy, d, nat, l_ref, True)
     kp_ref[3] = z_next(kp_ref[2])
-    for copy in copies[5:]:
+    for copy in copies[10:]:
         copy.wait()
     for level in range(visc_ref.shape[0]):
         visc_ref[pl.ds(level, 1), :] = jnp.full((1, z), levels[level], F32)
@@ -692,9 +694,8 @@
                 for b, value in enumerate(between(lines[0][a], lines[1][a])):
                     at = pl.ds(cells * (16 * c + 4 * a + b), cells)
                     held[d, at, :] = (r_ref[d, at, :] + value).astype(BF)
-            part = pl.ds(16 * cells * c, 16 * cells)
-            copies.append(pltpu.make_async_copy(held.at[d, part], out_hbm.at[d, part], sems.at[3 * d + c]))
-            copies[-1].start()
+        copies.append(pltpu.make_async_copy(held.at[d], out_hbm.at[d], sems.at[d]))
+        copies[d].start()
     for copy in copies:
         copy.wait()
 
@@ -743,7 +744,7 @@
         [
             y_message, y_message,
             vm((3, 48 * cells, z), BF), vm((3, cells, z), jnp.int32), vm((cells, z), jnp.int32),
-            pltpu.SMEM(viscosity.shape, F32), pltpu.SemaphoreType.DMA((8,)),
+            pltpu.SMEM(viscosity.shape, F32), pltpu.SemaphoreType.DMA((13,)),
         ],
         wx * per_hex, True,
     )
@@ -787,7 +788,7 @@
             visc, lifted, flags, parts, mx, ownx, residual, late, vs, inverse, v1, yd, yu, outer, inner,
         ),
         (jax.ShapeDtypeStruct((3, 48 * cells, z), BF), vm((3, 48 * cells, z), F32)),
-        [vm((3, 48 * cells, z), BF), vm((2, 4 * wy * (wx + 1), z), F32), pltpu.SemaphoreType.DMA((9,))], 6 * per_hex,
+        [vm((3, 48 * cells, z), BF), vm((2, 4 * wy * (wx + 1), z), F32), pltpu.SemaphoreType.DMA((3,))], 6 * per_hex,
         aliases={6: 1},
     )
     return out.reshape(traces.shape)

time: 14.3 us -> 14.3 us (level)
  no operation moved by 1% of the time
where the time goes in v1:
time: 14.3 us; the launch traced here: 14.1 us
  Pallas kernels  6.32 us (44%)
  starting transfers between devices  5.76 us (40%)
  waiting for transfers between devices  1.92 us (13%)
    pallas_call x5, Pallas kernels, call(): pl.pallas_call(body, **keywords, in_specs=[pl.BlockSpec(memory_space=pltp...  6.32 us
    ppermute x5, starting transfers between devices, swap(): lax.ppermute(value, ('gx', 'gy'), pairs + [(high, low) for low, high in p...  5.76 us
    ppermute x5, waiting for transfers between devices, swap(): lax.ppermute(value, ('gx', 'gy'), pairs + [(high, low) for low, high in p...  1.92 us
  transfers between devices with their start and end apart: 5, of which 1 were waited for; matrix products, arithmetic and copies ran while one was open for 0% of the time, Pallas kernels for 17%

profile of v1, /device:TPU:0, one launch (start us, length us, event | category | flops | bytes accessed | tf_op | source)
XLA Modules:
  0.0 14.1 jit_solution(12855642424323828541)
XLA Ops:
  0.0 2.2 %shard_map.82 = (bf16[4,16,48,128]{3,2,1,0:T(8,128)(2,1)S(1)}, f32[3,768,128]{2,1,0:T(8,128)S(1)}, f32[6,16,128]{2,1,0:T(8,128)S(1)}, f32[4,128]{1,0:T(4,128)S(1...) custom-call(f32[4]{0:T(128)} %visc_hbm.1, ...), custom_call_target="tpu_custom_call" | custom-call | flops 113246208 | bytes 1000000 | tf_op jit(solution)/shard_map/pallas_call | solution.py:710
  2.2 3.1 %collective-permute-start = (bf16[288,128]{1,0:T(8,128)(2,1)S(1)}, bf16[288,128]{1,0:T(8,128)(2,1)S(1)}, u32[]{:S(2)}, u32[]{:S(2)}) collective-permute-start(bf16[288,128]{1,0:T(8,128)(2,1)S(1)} %get-tuple-element.57), channel_id=1, source_target_pairs={{0,1},{4,5},{8,9},{12,13},{16,17},{20,21},{24,25},{28,29},{2,6},{1... | collective-permute-start | bytes 221192 | tf_op jit(solution)/shard_map/ppermute | solution.py:27
  5.3 0.0 collective-permute-start.1
  5.3 0.5 %collective-permute-start.2 = (bf16[288,128]{1,0:T(8,128)(2,1)S(1)}, bf16[288,128]{1,0:T(8,128)(2,1)S(1)}, u32[]{:S(2)}, u32[]{:S(2)}) collective-permute-start(bf16[288,128]{1,0:T(8,128)(2,1)S(1)} %get-tuple-element.59), channel_id=1, source_target_pairs={{2,3},{6,7},{10,11},{14,15},{18,19},{22,23},{26,27},{30,31},{0,4},... | collective-permute-start | bytes 221192 | tf_op jit(solution)/shard_map/ppermute | solution.py:27
  5.8 1.9 %shard_map.83 = (f32[6,16,48,128]{3,2,1,0:T(8,128)S(1)}, f32[2,5,8,128]{3,2,1,0:T(8,128)S(1)}, f32[2,16,128]{2,1,0:T(8,128)S(1)}, bf16[384,48]{1,0:T(8,128)(2,1)...) custom-call(bf16[4,16,48,128]{3,2,1,0:T(8,128)(2,1)S(1)} %get-tuple-element.41.l_ref, ...), custom_call_target="tpu_custom_call" | custom-call | flops 452984832 | bytes 1000000 | tf_op jit(solution)/shard_map/pallas_call | solution.py:710
  7.7 0.0 collective-permute-done.swap0_in
  7.7 0.0 collective-permute-done.1.swap1_in
  7.7 0.0 collective-permute-done.2.swap2_in
  7.7 0.3 %shard_map.84 = (f32[2,6,48,128]{3,2,1,0:T(8,128)S(1)}, f32[2,2,8,128]{3,2,1,0:T(8,128)S(1)}, f32[2,2,8,128]{3,2,1,0:T(8,128)S(1)}, f32[6,16,128]{2,1,0:T(8,128)...) custom-call(f32[4,128]{1,0:T(4,128)S(1)} %get-tuple-element.40.visc_, ...), custom_call_target="tpu_custom_call" | custom-call | flops 56623104 | bytes 1000000 | tf_op jit(solution)/shard_map/pallas_call | solution.py:710
  8.1 2.1 %collective-permute-start.3 = (bf16[336,128]{1,0:T(8,128)(2,1)S(1)}, bf16[336,128]{1,0:T(8,128)(2,1)S(1)}, u32[]{:S(2)}, u32[]{:S(2)}) collective-permute-start(bf16[336,128]{1,0:T(8,128)(2,1)S(1)} %get-tuple-element.72), channel_id=1, source_target_pairs={{4,8},{5,9},{6,10},{7,11},{12,16},{13,17},{14,18},{15,19},{20,24},... | collective-permute-start | bytes 258056 | tf_op jit(solution)/shard_map/ppermute | solution.py:27
  10.2 0.0 collective-permute-start.4
  10.2 0.5 %shard_map.85 = (f32[3,768,128]{2,1,0:T(8,128)S(1)}, f32[4,4,48,128]{3,2,1,0:T(8,128)S(1)}, f32[5,24,128]{2,1,0:T(8,128)S(1)}, f32[4,24,128]{2,1,0:T(8,128)S(1)}, f32[144,768]{1,0:T(8,128)S(1)}) custom-call(f32[4,128]{1,0:T(4,128)S(1)} %get-tuple-element.40.visc_ref, bf16[4,16,48,128]{3,2,1,0:T(8,128)(2,1)S(1)} %get-tuple-element.41.l_ref, ...), custom_call_target="tpu_custom_call" | custom-call | flops 113246208 | bytes 1000000 | tf_op jit(solution)/shard_map/pallas_call | solution.py:710
  10.8 1.9 %collective-permute-done.3.outer_in = bf16[336,128]{1,0:T(8,128)(2,1)S(1)} collective-permute-done((bf16[336,128]{1,0:T(8,128)(2,1)S(1)}, bf16[336,128]{1,0:T(8,128)(2,1)S(1)}, u32[]{:S(2)}, u32[]{:S(2)}) %collective-permute-start.3) | collective-permute-done | bytes 86048 | tf_op jit(solution)/shard_map/ppermute | solution.py:27
  12.7 0.0 collective-permute-done.4.inner_in
  12.7 1.4 %shard_map.86 = (bf16[3,768,128]{2,1,0:T(8,128)(2,1)}, f32[3,768,128]{2,1,0:T(8,128)S(1)}) custom-call(f32[4,128]{1,0:T(4,128)S(1)} %get-tuple-element.40.visc_ref, bf16[4,16,48,128]{3,2,1,0:T(8,128)(2,1)S(1)} %get-tuple-element.41.l_ref, f32[6,16,128]{2,1,0:T(8,128)S(1)} %get-tuple-element.42.kp_ref, ...), custom_call_target="tpu_custom_call", output_to_operand_aliasing={{1}: (6, {})} | custom-call | flops 169869312 | bytes 1000000 | tf_op jit(solution)/shard_map/pallas_call | solution.py:710
Async XLA Ops:
  2.2 5.5 %collective-permute-start = (bf16[288,128]{1,0:T(8,128)(2,1)S(1)}, bf16[288,128]{1,0:T(8,128)(2,1)S(1)}, u32[]{:S(2)}, u32[]{:S(2)}) collective-permute-start(bf16[288,128]{1,0:T(8,128)(2,1)S(1)} %get-tuple-element.57), channel_id=1, source_target_pairs={{0,1},{4,5},{8,9},{12,13},{16,17},{20,21},{24,25},{28,29},{2,6},{1... | collective-permute-start | bytes 221192 | tf_op jit(solution)/shard_map/ppermute | solution.py:27
  5.3 2.4 %collective-permute-start.1 = (bf16[288,128]{1,0:T(8,128)(2,1)S(1)}, bf16[288,128]{1,0:T(8,128)(2,1)S(1)}, u32[]{:S(2)}, u32[]{:S(2)}) collective-permute-start(bf16[288,128]{1,0:T(8,128)(2,1)S(1)} %get-tuple-element.58), channel_id=1, source_target_pairs={{1,2},{5,6},{9,10},{13,14},{17,18},{21,22},{25,26},{29,30},{0,4},{... | collective-permute-start | bytes 221192 | tf_op jit(solution)/shard_map/ppermute | solution.py:27
  5.3 2.4 %collective-permute-start.2 = (bf16[288,128]{1,0:T(8,128)(2,1)S(1)}, bf16[288,128]{1,0:T(8,128)(2,1)S(1)}, u32[]{:S(2)}, u32[]{:S(2)}) collective-permute-start(bf16[288,128]{1,0:T(8,128)(2,1)S(1)} %get-tuple-element.59), channel_id=1, source_target_pairs={{2,3},{6,7},{10,11},{14,15},{18,19},{22,23},{26,27},{30,31},{0,4},... | collective-permute-start | bytes 221192 | tf_op jit(solution)/shard_map/ppermute | solution.py:27
  8.1 4.6 %collective-permute-start.3 = (bf16[336,128]{1,0:T(8,128)(2,1)S(1)}, bf16[336,128]{1,0:T(8,128)(2,1)S(1)}, u32[]{:S(2)}, u32[]{:S(2)}) collective-permute-start(bf16[336,128]{1,0:T(8,128)(2,1)S(1)} %get-tuple-element.72), channel_id=1, source_target_pairs={{4,8},{5,9},{6,10},{7,11},{12,16},{13,17},{14,18},{15,19},{20,24},... | collective-permute-start | bytes 258056 | tf_op jit(solution)/shard_map/ppermute | solution.py:27
  10.2 2.5 %collective-permute-start.4 = (bf16[336,128]{1,0:T(8,128)(2,1)S(1)}, bf16[336,128]{1,0:T(8,128)(2,1)S(1)}, u32[]{:S(2)}, u32[]{:S(2)}) collective-permute-start(bf16[336,128]{1,0:T(8,128)(2,1)S(1)} %get-tuple-element.73), channel_id=1, source_target_pairs={{0,4},{1,5},{2,6},{3,7},{8,12},{9,13},{10,14},{11,15},{16,20},{17,... | collective-permute-start | bytes 258056 | tf_op jit(solution)/shard_map/ppermute | solution.py:27

commit v2 on v0

--- a/solution.py
+++ b/solution.py
@@ -99,6 +99,14 @@
 
 
 slot_rows = (0, 16, 32, 64, 96, 112, 128)
+
+
+def block_table():
+    slots = np.split(slot_table().astype(np.float64), slot_rows[1:6], axis=0)
+    table = np.zeros((96, 288), np.float64)
+    for s, first in enumerate((0, 16, 32, 32, 64, 80)):
+        table[first : first + len(slots[s]), 48 * s : 48 * s + 48] += slots[s]
+    return table.astype(ml_dtypes.bfloat16)
 
 
 def between(low, high):
@@ -204,24 +212,24 @@
 
 
 def first_kernel(
-    wx, wy, visc_hbm, t_hbm, dir_hbm, cls_hbm, diag_hbm, st_hbm, f_hbm, parts_hbm,
-    l_ref, nat, kp_ref, visc_ref, diag_ref, st_ref, f_ref, parts_ref, v_ref, v1_ref, v3_ref,
-    swap0_ref, swap1_ref, swap2_ref, down_ref, up_ref, t_ref, dir_ref, cls_ref, levels, sems,
+    wx, wy, visc_hbm, t_hbm, dir_hbm, cls_hbm, diag_hbm, st_hbm, f_hbm, block_hbm,
+    l_ref, nat, kp_ref, visc_ref, diag_ref, st_ref, f_ref, v_ref, v1_ref, v3_ref,
+    swap0_ref, swap1_ref, swap2_ref, down_ref, up_ref, block_ref, t_ref, dir_ref, cls_ref, levels, sems,
 ):
     cells = wx * wy
     pairs = [
-        (parts_hbm, parts_ref), (f_hbm, f_ref), (st_hbm, st_ref), (t_hbm, t_ref), (dir_hbm, dir_ref),
+        (block_hbm, block_ref), (f_hbm, f_ref), (st_hbm, st_ref), (t_hbm, t_ref), (dir_hbm, dir_ref),
         (cls_hbm, cls_ref), (visc_hbm, levels), (diag_hbm, diag_ref),
     ]
     copies = [pltpu.make_async_copy(a, b, sems.at[i]) for i, (a, b) in enumerate(pairs)]
     for copy in copies:
         copy.start()
-    diagonal = lax.broadcasted_iota(jnp.int32, (288, 288), 0) == lax.broadcasted_iota(jnp.int32, (288, 288), 1)
-    diagonal = jnp.where(diagonal, F32(penalty), F32(0.0))
     copies[0].wait()
-    own = tall([vertex_part(diagonal, parts_ref), diagonal[144:192]])
     copies[1].wait()
-    left = tall([vertex_part(f_ref[...], parts_ref).astype(BF), f_ref[pl.ds(144, 48), :]])
+    left = tall([dot(block_ref[...], f_ref[...]).astype(BF), f_ref[pl.ds(144, 48), :]])
+    place = lax.broadcasted_iota(jnp.int32, (48, 288), 0) + 144
+    diagonal = jnp.where(place == lax.broadcasted_iota(jnp.int32, (48, 288), 1), F32(penalty), F32(0.0))
+    own = tall([penalty * block_ref[...].astype(F32), diagonal])
     for copy in copies[2:5]:
         copy.wait()
     short = (turned_dot(left, st_ref[...]) + own).astype(BF)
@@ -692,9 +700,8 @@
                 for b, value in enumerate(between(lines[0][a], lines[1][a])):
                     at = pl.ds(cells * (16 * c + 4 * a + b), cells)
                     held[d, at, :] = (r_ref[d, at, :] + value).astype(BF)
-            part = pl.ds(16 * cells * c, 16 * cells)
-            copies.append(pltpu.make_async_copy(held.at[d, part], out_hbm.at[d, part], sems.at[3 * d + c]))
-            copies[-1].start()
+        copies.append(pltpu.make_async_copy(held.at[d], out_hbm.at[d], sems.at[d]))
+        copies[d].start()
     for copy in copies:
         copy.wait()
 
@@ -722,26 +729,26 @@
     cells = wx * wy
     rows = 8 * (wy // 2 + 1)
     per_hex = 2 * 384 * 288 * z
-    parts = jnp.asarray(slot_table())
+    parts, block = jnp.asarray(slot_table()), jnp.asarray(block_table())
     vm = pltpu.VMEM
     bind = lambda body: functools.partial(body, wx, wy)
     y_message = vm((48 * wx + 48 + tail_rows(8 * ((wx + 2) // 2) + 8 + 3 * wx + 4), z), BF)
     x_message = vm((48 * (wy + 2) + tail_rows(rows + 3 * wy + 4), z), BF)
 
-    (lifted, nat, flags, visc, diag, s_turned, f_map, parts, va, v1a, v3, *swaps) = call(
+    (lifted, nat, flags, visc, diag, s_turned, f_map, va, v1a, v3, *swaps) = call(
         bind(first_kernel),
         (
             viscosity, traces.reshape(3, 48 * cells, z), dirichlet.reshape(3, cells, z),
-            visc_class.reshape(cells, z), coarse_diag.reshape(cells, z), solve_map.T, flux_map, parts,
+            visc_class.reshape(cells, z), coarse_diag.reshape(cells, z), solve_map.T, flux_map, block,
         ),
         (
             vm((4, cells, 48, z), BF), vm((3, 48 * cells, z), F32), vm((6, cells, z), F32), vm((viscosity.shape[0], z), F32), vm((cells, z), F32),
-            vm(solve_map.shape[::-1], BF), vm(flux_map.shape, BF), vm(parts.shape, BF),
+            vm(solve_map.shape[::-1], BF), vm(flux_map.shape, BF),
             vm((2, wx + 1, 8, z), F32), vm((2, 16, z), F32), vm((wx, 32, z), F32),
             y_message, y_message, y_message,
         ),
         [
-            y_message, y_message,
+            y_message, y_message, vm(block.shape, BF),
             vm((3, 48 * cells, z), BF), vm((3, cells, z), jnp.int32), vm((cells, z), jnp.int32),
             pltpu.SMEM(viscosity.shape, F32), pltpu.SemaphoreType.DMA((8,)),
         ],
@@ -787,7 +794,7 @@
             visc, lifted, flags, parts, mx, ownx, residual, late, vs, inverse, v1, yd, yu, outer, inner,
         ),
         (jax.ShapeDtypeStruct((3, 48 * cells, z), BF), vm((3, 48 * cells, z), F32)),
-        [vm((3, 48 * cells, z), BF), vm((2, 4 * wy * (wx + 1), z), F32), pltpu.SemaphoreType.DMA((9,))], 6 * per_hex,
+        [vm((3, 48 * cells, z), BF), vm((2, 4 * wy * (wx + 1), z), F32), pltpu.SemaphoreType.DMA((3,))], 6 * per_hex,
         aliases={6: 1},
     )
     return out.reshape(traces.shape)

time: 14.3 us -> 14.9 us (1.042)
  local copies, waits for them, and re-layouts: 0 us -> 0.76 us
  starting transfers between devices: 5.74 us -> 5.27 us
  waiting for transfers between devices: 1.92 us -> 2.34 us
    unnamed x0 -> x4, local copies, waits for them, and re-layouts: none -> 0.76 us
    ppermute x5, starting transfers between devices: 5.74 us -> 5.27 us  [swap(): lax.ppermute(value, ('gx', 'gy'), pairs + [(high, low) for low, high in p...]
    ppermute x5, waiting for transfers between devices: 1.92 us -> 2.34 us  [swap(): lax.ppermute(value, ('gx', 'gy'), pairs + [(high, low) for low, high in p...]
  transfers between devices with their start and end apart: 5 -> 5, of which waited for: 1 -> 1; matrix products, arithmetic and copies ran while one was open for 0% -> 0% of each run, Pallas kernels for 17% -> 16%
where the time goes in v2:
time: 14.9 us; the launch traced here: 14.7 us
  Pallas kernels  6.27 us (42%)
  starting transfers between devices  5.27 us (35%)
  waiting for transfers between devices  2.34 us (16%)
  local copies, waits for them, and re-layouts  0.76 us (5%)
    pallas_call x5, Pallas kernels, call(): pl.pallas_call(body, **keywords, in_specs=[pl.BlockSpec(memory_space=pltp...  6.27 us
    ppermute x5, starting transfers between devices, swap(): lax.ppermute(value, ('gx', 'gy'), pairs + [(high, low) for low, high in p...  5.27 us
    ppermute x5, waiting for transfers between devices, swap(): lax.ppermute(value, ('gx', 'gy'), pairs + [(high, low) for low, high in p...  2.34 us
    unnamed x4, local copies, waits for them, and re-layouts  0.76 us
  transfers between devices with their start and end apart: 5, of which 1 were waited for; matrix products, arithmetic and copies ran while one was open for 0% of the time, Pallas kernels for 16%

profile of v2, /device:TPU:0, one launch (start us, length us, event | category | flops | bytes accessed | tf_op | source)
XLA Modules:
  0.0 14.7 jit_solution(209872848193649040)
XLA Ops:
  0.0 2.2 %shard_map.91 = (bf16[4,16,48,128]{3,2,1,0:T(8,128)(2,1)S(1)}, f32[3,768,128]{2,1,0:T(8,128)S(1)}, f32[6,16,128]{2,1,0:T(8,128)S(1)}, f32[4,128]{1,0:T(4,128)S(1...) custom-call(f32[4]{0:T(128)} %visc_hbm.1, ...), custom_call_target="tpu_custom_call" | custom-call | flops 113246208 | bytes 1000000 | tf_op jit(solution)/shard_map/pallas_call | solution.py:716
  2.2 3.1 %collective-permute-start = (bf16[288,128]{1,0:T(8,128)(2,1)S(1)}, bf16[288,128]{1,0:T(8,128)(2,1)S(1)}, u32[]{:S(2)}, u32[]{:S(2)}) collective-permute-start(bf16[288,128]{1,0:T(8,128)(2,1)S(1)} %get-tuple-element.55), channel_id=1, source_target_pairs={{0,1},{4,5},{8,9},{12,13},{16,17},{20,21},{24,25},{28,29},{2,6},{1... | collective-permute-start | bytes 221192 | tf_op jit(solution)/shard_map/ppermute | solution.py:27
  5.3 0.0 collective-permute-start.1
  5.3 0.5 %collective-permute-start.2 = (bf16[288,128]{1,0:T(8,128)(2,1)S(1)}, bf16[288,128]{1,0:T(8,128)(2,1)S(1)}, u32[]{:S(2)}, u32[]{:S(2)}) collective-permute-start(bf16[288,128]{1,0:T(8,128)(2,1)S(1)} %get-tuple-element.57), channel_id=1, source_target_pairs={{2,3},{6,7},{10,11},{14,15},{18,19},{22,23},{26,27},{30,31},{0,4},... | collective-permute-start | bytes 221192 | tf_op jit(solution)/shard_map/ppermute | solution.py:27
  5.8 0.0 copy-start
  5.8 0.8 %copy-done = bf16[128,48]{1,0:T(8,128)(2,1)S(1)} copy-done((bf16[128,48]{1,0:T(8,128)(2,1)S(1)}, bf16[128,48]{1,0:T(8,128)(2,1)}, u32[]{:S(2)}) %copy-start) | copy-done | bytes 12312
  6.5 1.9 %shard_map.92 = (f32[6,16,48,128]{3,2,1,0:T(8,128)S(1)}, f32[2,5,8,128]{3,2,1,0:T(8,128)S(1)}, f32[2,16,128]{2,1,0:T(8,128)S(1)}, bf16[384,48]{1,0:T(8,128)(2,1)...) custom-call(bf16[4,16,48,128]{3,2,1,0:T(8,128)(2,1)S(1)} %get-tuple-element.40.l_ref, ...), custom_call_target="tpu_custom_call" | custom-call | flops 452984832 | bytes 1000000 | tf_op jit(solution)/shard_map/pallas_call | solution.py:716
  8.4 0.0 collective-permute-done.swap0_in
  8.4 0.0 collective-permute-done.1.swap1_in
  8.4 0.0 collective-permute-done.2.swap2_in
  8.4 0.0 copy-start.1
  8.4 0.3 %shard_map.93 = (f32[2,6,48,128]{3,2,1,0:T(8,128)S(1)}, f32[2,2,8,128]{3,2,1,0:T(8,128)S(1)}, f32[2,2,8,128]{3,2,1,0:T(8,128)S(1)}, f32[6,16,128]{2,1,0:T(8,128)...) custom-call(f32[4,128]{1,0:T(4,128)S(1)} %get-tuple-element.39.visc_, ...), custom_call_target="tpu_custom_call" | custom-call | flops 56623104 | bytes 1000000 | tf_op jit(solution)/shard_map/pallas_call | solution.py:716
  8.8 1.4 %collective-permute-start.3 = (bf16[336,128]{1,0:T(8,128)(2,1)S(1)}, bf16[336,128]{1,0:T(8,128)(2,1)S(1)}, u32[]{:S(2)}, u32[]{:S(2)}) collective-permute-start(bf16[336,128]{1,0:T(8,128)(2,1)S(1)} %get-tuple-element.70), channel_id=1, source_target_pairs={{4,8},{5,9},{6,10},{7,11},{12,16},{13,17},{14,18},{15,19},{20,24},... | collective-permute-start | bytes 258056 | tf_op jit(solution)/shard_map/ppermute | solution.py:27
  10.2 0.3 %collective-permute-start.4 = (bf16[336,128]{1,0:T(8,128)(2,1)S(1)}, bf16[336,128]{1,0:T(8,128)(2,1)S(1)}, u32[]{:S(2)}, u32[]{:S(2)}) collective-permute-start(bf16[336,128]{1,0:T(8,128)(2,1)S(1)} %get-tuple-element.71), channel_id=1, source_target_pairs={{0,4},{1,5},{2,6},{3,7},{8,12},{9,13},{10,14},{11,15},{16,20},{17,... | collective-permute-start | bytes 258056 | tf_op jit(solution)/shard_map/ppermute | solution.py:27
  10.5 0.0 copy-done.1
  10.5 0.5 %shard_map.94 = (f32[3,768,128]{2,1,0:T(8,128)S(1)}, f32[4,4,48,128]{3,2,1,0:T(8,128)S(1)}, f32[5,24,128]{2,1,0:T(8,128)S(1)}, f32[4,24,128]{2,1,0:T(8,128)S(1)}, f32[144,768]{1,0:T(8,128)S(1)}) custom-call(f32[4,128]{1,0:T(4,128)S(1)} %get-tuple-element.39.visc_ref, bf16[4,16,48,128]{3,2,1,0:T(8,128)(2,1)S(1)} %get-tuple-element.40.l_ref, ...), custom_call_target="tpu_custom_call" | custom-call | flops 113246208 | bytes 1000000 | tf_op jit(solution)/shard_map/pallas_call | solution.py:716
  11.0 2.3 %collective-permute-done.3.outer_in = bf16[336,128]{1,0:T(8,128)(2,1)S(1)} collective-permute-done((bf16[336,128]{1,0:T(8,128)(2,1)S(1)}, bf16[336,128]{1,0:T(8,128)(2,1)S(1)}, u32[]{:S(2)}, u32[]{:S(2)}) %collective-permute-start.3) | collective-permute-done | bytes 86048 | tf_op jit(solution)/shard_map/ppermute | solution.py:27
  13.3 0.0 collective-permute-done.4.inner_in
  13.3 1.4 %shard_map.95 = (bf16[3,768,128]{2,1,0:T(8,128)(2,1)}, f32[3,768,128]{2,1,0:T(8,128)S(1)}) custom-call(f32[4,128]{1,0:T(4,128)S(1)} %get-tuple-element.39.visc_ref, bf16[4,16,48,128]{3,2,1,0:T(8,128)(2,1)S(1)} %get-tuple-element.40.l_ref, f32[6,16,128]{2,1,0:T(8,128)S(1)} %get-tuple-element.41.kp_ref, ...), custom_call_target="tpu_custom_call", output_to_operand_aliasing={{1}: (6, {})} | custom-call | flops 169869312 | bytes 1000000 | tf_op jit(solution)/shard_map/pallas_call | solution.py:716
Async XLA Ops:
  2.2 6.2 %collective-permute-start = (bf16[288,128]{1,0:T(8,128)(2,1)S(1)}, bf16[288,128]{1,0:T(8,128)(2,1)S(1)}, u32[]{:S(2)}, u32[]{:S(2)}) collective-permute-start(bf16[288,128]{1,0:T(8,128)(2,1)S(1)} %get-tuple-element.55), channel_id=1, source_target_pairs={{0,1},{4,5},{8,9},{12,13},{16,17},{20,21},{24,25},{28,29},{2,6},{1... | collective-permute-start | bytes 221192 | tf_op jit(solution)/shard_map/ppermute | solution.py:27
  5.3 3.2 %collective-permute-start.1 = (bf16[288,128]{1,0:T(8,128)(2,1)S(1)}, bf16[288,128]{1,0:T(8,128)(2,1)S(1)}, u32[]{:S(2)}, u32[]{:S(2)}) collective-permute-start(bf16[288,128]{1,0:T(8,128)(2,1)S(1)} %get-tuple-element.56), channel_id=1, source_target_pairs={{1,2},{5,6},{9,10},{13,14},{17,18},{21,22},{25,26},{29,30},{0,4},{... | collective-permute-start | bytes 221192 | tf_op jit(solution)/shard_map/ppermute | solution.py:27
  5.3 3.2 %collective-permute-start.2 = (bf16[288,128]{1,0:T(8,128)(2,1)S(1)}, bf16[288,128]{1,0:T(8,128)(2,1)S(1)}, u32[]{:S(2)}, u32[]{:S(2)}) collective-permute-start(bf16[288,128]{1,0:T(8,128)(2,1)S(1)} %get-tuple-element.57), channel_id=1, source_target_pairs={{2,3},{6,7},{10,11},{14,15},{18,19},{22,23},{26,27},{30,31},{0,4},... | collective-permute-start | bytes 221192 | tf_op jit(solution)/shard_map/ppermute | solution.py:27
  5.8 0.8 %copy-start = (bf16[128,48]{1,0:T(8,128)(2,1)S(1)}, bf16[128,48]{1,0:T(8,128)(2,1)}, u32[]{:S(2)}) copy-start(bf16[128,48]{1,0:T(8,128)(2,1)} %constant.4.clone.parts_ref) | copy-start | bytes 36868
  8.4 2.0 %copy-start.1 = (bf16[128,48]{1,0:T(8,128)(2,1)S(1)}, bf16[128,48]{1,0:T(8,128)(2,1)}, u32[]{:S(2)}) copy-start(bf16[128,48]{1,0:T(8,128)(2,1)} %constant.4.clone.parts_ref) | copy-start | bytes 36868
  8.8 4.5 %collective-permute-start.3 = (bf16[336,128]{1,0:T(8,128)(2,1)S(1)}, bf16[336,128]{1,0:T(8,128)(2,1)S(1)}, u32[]{:S(2)}, u32[]{:S(2)}) collective-permute-start(bf16[336,128]{1,0:T(8,128)(2,1)S(1)} %get-tuple-element.70), channel_id=1, source_target_pairs={{4,8},{5,9},{6,10},{7,11},{12,16},{13,17},{14,18},{15,19},{20,24},... | collective-permute-start | bytes 258056 | tf_op jit(solution)/shard_map/ppermute | solution.py:27
  10.2 3.2 %collective-permute-start.4 = (bf16[336,128]{1,0:T(8,128)(2,1)S(1)}, bf16[336,128]{1,0:T(8,128)(2,1)S(1)}, u32[]{:S(2)}, u32[]{:S(2)}) collective-permute-start(bf16[336,128]{1,0:T(8,128)(2,1)S(1)} %get-tuple-element.71), channel_id=1, source_target_pairs={{0,4},{1,5},{2,6},{3,7},{8,12},{9,13},{10,14},{11,15},{16,20},{17,... | collective-permute-start | bytes 258056 | tf_op jit(solution)/shard_map/ppermute | solution.py:27

commit v3 on v0

--- a/solution.py
+++ b/solution.py
@@ -227,11 +227,9 @@
     short = (turned_dot(left, st_ref[...]) + own).astype(BF)
     z = t_ref.shape[2]
     for d in range(3):
-        keep = (1 - dir_ref[d]).astype(F32)
-        kp_ref[d] = keep
-        masked = t_ref[d].astype(F32).reshape(48, cells, z) * keep[None]
-        nat[d] = masked.reshape(48 * cells, z)
-        lay_out(wx, wy, d, nat, l_ref, True)
+        kp_ref[d] = (1 - dir_ref[d]).astype(F32)
+        nat[d] = t_ref[d].astype(F32)
+        lay_out(wx, wy, d, nat, kp_ref, l_ref, True)
     kp_ref[3] = z_next(kp_ref[2])
     for copy in copies[5:]:
         copy.wait()
@@ -323,12 +321,12 @@
     return y in (0, wy - 1) or (d == 0 and x == 0) or (d == 1 and y == 1)
 
 
-def lay_out(wx, wy, d, nat, l_ref, first):
+def lay_out(wx, wy, d, nat, kp_ref, l_ref, first):
     for x in range(wx):
         for y in range(wy):
             if early(wx, wy, d, x, y) == first:
                 col = x * wy + y
-                part = nat[d, pl.ds(col, 48, stride=wx * wy), :]
+                part = nat[d, pl.ds(col, 48, stride=wx * wy), :] * kp_ref[d, pl.ds(col, 1), :]
                 l_ref[d, col] = part.astype(BF)
                 if d == 2:
                     l_ref[3, col] = z_next(part).astype(BF)
@@ -383,7 +381,7 @@
     m_ref[pl.ds(288, 96), :] = vertex_part(flux, parts_ref).astype(BF)
     lost_ref[...] = (flux - flux.astype(BF).astype(F32))[:, 0:256].astype(BF)
     for d in range(3):
-        lay_out(wx, wy, d, nat, rest_ref, False)
+        lay_out(wx, wy, d, nat, kp_ref, rest_ref, False)
     own_ref[...] = dot(
         tall([my_ref[pl.ds(144, 48), :], my_ref[pl.ds(288, 96), :]]), wide([l_ref[1, x * wy] for x in range(wx)])
     )
@@ -692,9 +690,8 @@
                 for b, value in enumerate(between(lines[0][a], lines[1][a])):
                     at = pl.ds(cells * (16 * c + 4 * a + b), cells)
                     held[d, at, :] = (r_ref[d, at, :] + value).astype(BF)
-            part = pl.ds(16 * cells * c, 16 * cells)
-            copies.append(pltpu.make_async_copy(held.at[d, part], out_hbm.at[d, part], sems.at[3 * d + c]))
-            copies[-1].start()
+        copies.append(pltpu.make_async_copy(held.at[d], out_hbm.at[d], sems.at[d]))
+        copies[d].start()
     for copy in copies:
         copy.wait()
 
@@ -787,7 +784,7 @@
             visc, lifted, flags, parts, mx, ownx, residual, late, vs, inverse, v1, yd, yu, outer, inner,
         ),
         (jax.ShapeDtypeStruct((3, 48 * cells, z), BF), vm((3, 48 * cells, z), F32)),
-        [vm((3, 48 * cells, z), BF), vm((2, 4 * wy * (wx + 1), z), F32), pltpu.SemaphoreType.DMA((9,))], 6 * per_hex,
+        [vm((3, 48 * cells, z), BF), vm((2, 4 * wy * (wx + 1), z), F32), pltpu.SemaphoreType.DMA((3,))], 6 * per_hex,
         aliases={6: 1},
     )
     return out.reshape(traces.shape)

time: 14.3 us -> 14.3 us (level)
  no operation moved by 1% of the time
where the time goes in v3:
time: 14.3 us; the launch traced here: 14.1 us
  Pallas kernels  6.32 us (44%)
  starting transfers between devices  5.76 us (40%)
  waiting for transfers between devices  1.92 us (13%)
    pallas_call x5, Pallas kernels, call(): pl.pallas_call(body, **keywords, in_specs=[pl.BlockSpec(memory_space=pltp...  6.32 us
    ppermute x5, starting transfers between devices, swap(): lax.ppermute(value, ('gx', 'gy'), pairs + [(high, low) for low, high in p...  5.76 us
    ppermute x5, waiting for transfers between devices, swap(): lax.ppermute(value, ('gx', 'gy'), pairs + [(high, low) for low, high in p...  1.92 us
  transfers between devices with their start and end apart: 5, of which 1 were waited for; matrix products, arithmetic and copies ran while one was open for 0% of the time, Pallas kernels for 17%

profile of v3, /device:TPU:0, one launch (start us, length us, event | category | flops | bytes accessed | tf_op | source)
XLA Modules:
  0.0 14.1 jit_solution(10592433310157441174)
XLA Ops:
  0.0 2.2 %shard_map.82 = (bf16[4,16,48,128]{3,2,1,0:T(8,128)(2,1)S(1)}, f32[3,768,128]{2,1,0:T(8,128)S(1)}, f32[6,16,128]{2,1,0:T(8,128)S(1)}, f32[4,128]{1,0:T(4,128)S(1...) custom-call(f32[4]{0:T(128)} %visc_hbm.1, ...), custom_call_target="tpu_custom_call" | custom-call | flops 113246208 | bytes 1000000 | tf_op jit(solution)/shard_map/pallas_call | solution.py:706
  2.2 3.1 %collective-permute-start = (bf16[288,128]{1,0:T(8,128)(2,1)S(1)}, bf16[288,128]{1,0:T(8,128)(2,1)S(1)}, u32[]{:S(2)}, u32[]{:S(2)}) collective-permute-start(bf16[288,128]{1,0:T(8,128)(2,1)S(1)} %get-tuple-element.57), channel_id=1, source_target_pairs={{0,1},{4,5},{8,9},{12,13},{16,17},{20,21},{24,25},{28,29},{2,6},{1... | collective-permute-start | bytes 221192 | tf_op jit(solution)/shard_map/ppermute | solution.py:27
  5.3 0.0 collective-permute-start.1
  5.3 0.5 %collective-permute-start.2 = (bf16[288,128]{1,0:T(8,128)(2,1)S(1)}, bf16[288,128]{1,0:T(8,128)(2,1)S(1)}, u32[]{:S(2)}, u32[]{:S(2)}) collective-permute-start(bf16[288,128]{1,0:T(8,128)(2,1)S(1)} %get-tuple-element.59), channel_id=1, source_target_pairs={{2,3},{6,7},{10,11},{14,15},{18,19},{22,23},{26,27},{30,31},{0,4},... | collective-permute-start | bytes 221192 | tf_op jit(solution)/shard_map/ppermute | solution.py:27
  5.8 1.9 %shard_map.83 = (f32[6,16,48,128]{3,2,1,0:T(8,128)S(1)}, f32[2,5,8,128]{3,2,1,0:T(8,128)S(1)}, f32[2,16,128]{2,1,0:T(8,128)S(1)}, bf16[384,48]{1,0:T(8,128)(2,1)...) custom-call(bf16[4,16,48,128]{3,2,1,0:T(8,128)(2,1)S(1)} %get-tuple-element.41.l_ref, ...), custom_call_target="tpu_custom_call" | custom-call | flops 452984832 | bytes 1000000 | tf_op jit(solution)/shard_map/pallas_call | solution.py:706
  7.7 0.0 collective-permute-done.swap0_in
  7.7 0.0 collective-permute-done.1.swap1_in
  7.7 0.0 collective-permute-done.2.swap2_in
  7.7 0.3 %shard_map.84 = (f32[2,6,48,128]{3,2,1,0:T(8,128)S(1)}, f32[2,2,8,128]{3,2,1,0:T(8,128)S(1)}, f32[2,2,8,128]{3,2,1,0:T(8,128)S(1)}, f32[6,16,128]{2,1,0:T(8,128)...) custom-call(f32[4,128]{1,0:T(4,128)S(1)} %get-tuple-element.40.visc_, ...), custom_call_target="tpu_custom_call" | custom-call | flops 56623104 | bytes 1000000 | tf_op jit(solution)/shard_map/pallas_call | solution.py:706
  8.1 2.1 %collective-permute-start.3 = (bf16[336,128]{1,0:T(8,128)(2,1)S(1)}, bf16[336,128]{1,0:T(8,128)(2,1)S(1)}, u32[]{:S(2)}, u32[]{:S(2)}) collective-permute-start(bf16[336,128]{1,0:T(8,128)(2,1)S(1)} %get-tuple-element.72), channel_id=1, source_target_pairs={{4,8},{5,9},{6,10},{7,11},{12,16},{13,17},{14,18},{15,19},{20,24},... | collective-permute-start | bytes 258056 | tf_op jit(solution)/shard_map/ppermute | solution.py:27
  10.2 0.0 collective-permute-start.4
  10.2 0.5 %shard_map.85 = (f32[3,768,128]{2,1,0:T(8,128)S(1)}, f32[4,4,48,128]{3,2,1,0:T(8,128)S(1)}, f32[5,24,128]{2,1,0:T(8,128)S(1)}, f32[4,24,128]{2,1,0:T(8,128)S(1)}, f32[144,768]{1,0:T(8,128)S(1)}) custom-call(f32[4,128]{1,0:T(4,128)S(1)} %get-tuple-element.40.visc_ref, bf16[4,16,48,128]{3,2,1,0:T(8,128)(2,1)S(1)} %get-tuple-element.41.l_ref, ...), custom_call_target="tpu_custom_call" | custom-call | flops 113246208 | bytes 1000000 | tf_op jit(solution)/shard_map/pallas_call | solution.py:706
  10.8 1.9 %collective-permute-done.3.outer_in = bf16[336,128]{1,0:T(8,128)(2,1)S(1)} collective-permute-done((bf16[336,128]{1,0:T(8,128)(2,1)S(1)}, bf16[336,128]{1,0:T(8,128)(2,1)S(1)}, u32[]{:S(2)}, u32[]{:S(2)}) %collective-permute-start.3) | collective-permute-done | bytes 86048 | tf_op jit(solution)/shard_map/ppermute | solution.py:27
  12.7 0.0 collective-permute-done.4.inner_in
  12.7 1.4 %shard_map.86 = (bf16[3,768,128]{2,1,0:T(8,128)(2,1)}, f32[3,768,128]{2,1,0:T(8,128)S(1)}) custom-call(f32[4,128]{1,0:T(4,128)S(1)} %get-tuple-element.40.visc_ref, bf16[4,16,48,128]{3,2,1,0:T(8,128)(2,1)S(1)} %get-tuple-element.41.l_ref, f32[6,16,128]{2,1,0:T(8,128)S(1)} %get-tuple-element.42.kp_ref, ...), custom_call_target="tpu_custom_call", output_to_operand_aliasing={{1}: (6, {})} | custom-call | flops 169869312 | bytes 1000000 | tf_op jit(solution)/shard_map/pallas_call | solution.py:706
Async XLA Ops:
  2.2 5.5 %collective-permute-start = (bf16[288,128]{1,0:T(8,128)(2,1)S(1)}, bf16[288,128]{1,0:T(8,128)(2,1)S(1)}, u32[]{:S(2)}, u32[]{:S(2)}) collective-permute-start(bf16[288,128]{1,0:T(8,128)(2,1)S(1)} %get-tuple-element.57), channel_id=1, source_target_pairs={{0,1},{4,5},{8,9},{12,13},{16,17},{20,21},{24,25},{28,29},{2,6},{1... | collective-permute-start | bytes 221192 | tf_op jit(solution)/shard_map/ppermute | solution.py:27
  5.3 2.4 %collective-permute-start.1 = (bf16[288,128]{1,0:T(8,128)(2,1)S(1)}, bf16[288,128]{1,0:T(8,128)(2,1)S(1)}, u32[]{:S(2)}, u32[]{:S(2)}) collective-permute-start(bf16[288,128]{1,0:T(8,128)(2,1)S(1)} %get-tuple-element.58), channel_id=1, source_target_pairs={{1,2},{5,6},{9,10},{13,14},{17,18},{21,22},{25,26},{29,30},{0,4},{... | collective-permute-start | bytes 221192 | tf_op jit(solution)/shard_map/ppermute | solution.py:27
  5.3 2.4 %collective-permute-start.2 = (bf16[288,128]{1,0:T(8,128)(2,1)S(1)}, bf16[288,128]{1,0:T(8,128)(2,1)S(1)}, u32[]{:S(2)}, u32[]{:S(2)}) collective-permute-start(bf16[288,128]{1,0:T(8,128)(2,1)S(1)} %get-tuple-element.59), channel_id=1, source_target_pairs={{2,3},{6,7},{10,11},{14,15},{18,19},{22,23},{26,27},{30,31},{0,4},... | collective-permute-start | bytes 221192 | tf_op jit(solution)/shard_map/ppermute | solution.py:27
  8.1 4.6 %collective-permute-start.3 = (bf16[336,128]{1,0:T(8,128)(2,1)S(1)}, bf16[336,128]{1,0:T(8,128)(2,1)S(1)}, u32[]{:S(2)}, u32[]{:S(2)}) collective-permute-start(bf16[336,128]{1,0:T(8,128)(2,1)S(1)} %get-tuple-element.72), channel_id=1, source_target_pairs={{4,8},{5,9},{6,10},{7,11},{12,16},{13,17},{14,18},{15,19},{20,24},... | collective-permute-start | bytes 258056 | tf_op jit(solution)/shard_map/ppermute | solution.py:27
  10.2 2.5 %collective-permute-start.4 = (bf16[336,128]{1,0:T(8,128)(2,1)S(1)}, bf16[336,128]{1,0:T(8,128)(2,1)S(1)}, u32[]{:S(2)}, u32[]{:S(2)}) collective-permute-start(bf16[336,128]{1,0:T(8,128)(2,1)S(1)} %get-tuple-element.73), channel_id=1, source_target_pairs={{0,4},{1,5},{2,6},{3,7},{8,12},{9,13},{10,14},{11,15},{16,20},{17,... | collective-permute-start | bytes 258056 | tf_op jit(solution)/shard_map/ppermute | solution.py:27

commit v4 on v3

--- a/solution.py
+++ b/solution.py
@@ -227,9 +227,11 @@
     short = (turned_dot(left, st_ref[...]) + own).astype(BF)
     z = t_ref.shape[2]
     for d in range(3):
-        kp_ref[d] = (1 - dir_ref[d]).astype(F32)
-        nat[d] = t_ref[d].astype(F32)
-        lay_out(wx, wy, d, nat, kp_ref, l_ref, True)
+        keep = (1 - dir_ref[d]).astype(F32)
+        kp_ref[d] = keep
+        masked = t_ref[d].astype(F32).reshape(48, cells, z) * keep[None]
+        nat[d] = masked.reshape(48 * cells, z)
+    laid = lay_out(wx, wy, nat, l_ref, True)
     kp_ref[3] = z_next(kp_ref[2])
     for copy in copies[5:]:
         copy.wait()
@@ -242,7 +244,7 @@
     corners = []
     for side, y in enumerate((0, wy - 1)):
         where = [(x, y) for x in range(wx)]
-        slots, scales, left_out = known_hexes(wx, wy, where, (l_ref, None), kp_ref)
+        slots, scales, left_out = known_hexes(wx, wy, where, l_ref, laid, kp_ref)
         rows = columns(dot(short if side else short[0:96], elements(slots)), wx)
         corners += known_corners(rows, scales, left_out)
         v1_ref[side] = rows[wx - 1][16:32] * row(4, (wx - 1) * wy + y)
@@ -257,10 +259,10 @@
     corner = (wx - 1) * wy
     top = wy - 1
     for x in range(wx):
-        down_ref[pl.ds(48 * x, 48), :] = l_ref[1, x * wy]
+        down_ref[pl.ds(48 * x, 48), :] = laid[1, x, 0]
         up_ref[pl.ds(48 * x, 48), :] = lone[x][96:144].astype(BF)
-    down_ref[pl.ds(48 * wx, 48), :] = l_ref[0, 0]
-    up_ref[pl.ds(48 * wx, 48), :] = l_ref[0, top]
+    down_ref[pl.ds(48 * wx, 48), :] = laid[0, 0, 0]
+    up_ref[pl.ds(48 * wx, 48), :] = laid[0, 0, top]
     flags = [row(1, x * wy) for x in range(wx)] + [row(0, 0), row(5, corner), row(0, corner), row(2, corner)]
     diag = tall([diag_ref[pl.ds(x * wy, 1), :] for x in range(wx)])
     high = diag.astype(BF).astype(F32)
@@ -321,22 +323,26 @@
     return y in (0, wy - 1) or (d == 0 and x == 0) or (d == 1 and y == 1)
 
 
-def lay_out(wx, wy, d, nat, kp_ref, l_ref, first):
-    for x in range(wx):
-        for y in range(wy):
-            if early(wx, wy, d, x, y) == first:
-                col = x * wy + y
-                part = nat[d, pl.ds(col, 48, stride=wx * wy), :] * kp_ref[d, pl.ds(col, 1), :]
-                l_ref[d, col] = part.astype(BF)
-                if d == 2:
-                    l_ref[3, col] = z_next(part).astype(BF)
-
-
-def known_hexes(wx, wy, where, l_refs, kp_ref):
-    z = l_refs[0].shape[3]
+def lay_out(wx, wy, nat, l_ref, first):
+    laid = {}
+    for d in range(3):
+        for x in range(wx):
+            for y in range(wy):
+                if early(wx, wy, d, x, y) == first:
+                    part = nat[d, pl.ds(x * wy + y, 48, stride=wx * wy), :]
+                    laid[d, x, y] = part.astype(BF)
+                    if d == 2:
+                        laid[3, x, y] = z_next(part).astype(BF)
+    for (d, x, y), part in laid.items():
+        l_ref[d, x * wy + y] = part
+    return laid
+
+
+def known_hexes(wx, wy, where, l_ref, laid, kp_ref):
+    z = l_ref.shape[3]
     nothing = jnp.zeros((48, z), BF)
     row = lambda i, col: kp_ref[i, pl.ds(col, 1), :]
-    trace = lambda d, x, y: l_refs[0 if early(wx, wy, min(d, 2), x, y) else 1][d, x * wy + y]
+    trace = lambda d, x, y: laid[d, x, y] if (d, x, y) in laid else l_ref[d, x * wy + y]
     slots, scales, left_out = [], [], []
     for x, y in where:
         here = x * wy + y
@@ -380,15 +386,14 @@
     m_ref[pl.ds(0, 288), :] = flux.astype(BF)
     m_ref[pl.ds(288, 96), :] = vertex_part(flux, parts_ref).astype(BF)
     lost_ref[...] = (flux - flux.astype(BF).astype(F32))[:, 0:256].astype(BF)
-    for d in range(3):
-        lay_out(wx, wy, d, nat, kp_ref, rest_ref, False)
+    laid = lay_out(wx, wy, nat, rest_ref, False)
     own_ref[...] = dot(
         tall([my_ref[pl.ds(144, 48), :], my_ref[pl.ds(288, 96), :]]), wide([l_ref[1, x * wy] for x in range(wx)])
     )
     for y in range(wy):
         inside = 0 < y < wy - 1
         where = [(x, y) for x in range(wx)]
-        slots, scales, left_out = known_hexes(wx, wy, where, (l_ref, rest_ref), kp_ref)
+        slots, scales, left_out = known_hexes(wx, wy, where, l_ref, laid, kp_ref)
         element = elements(slots)
         rows = dot(m_ref[...] if inside else m_ref[pl.ds(0, 288), :], element)
         lost = columns(dot(lost_ref[...], element[0:256]), wx)

time: 14.3 us -> 14.3 us (level)
  no operation moved by 1% of the time
where the time goes in v4:
time: 14.3 us; the launch traced here: 14.1 us
  Pallas kernels  6.28 us (44%)
  starting transfers between devices  5.79 us (40%)
  waiting for transfers between devices  1.92 us (13%)
    pallas_call x5, Pallas kernels, call(): pl.pallas_call(body, **keywords, in_specs=[pl.BlockSpec(memory_space=pltp...  6.28 us
    ppermute x5, starting transfers between devices, swap(): lax.ppermute(value, ('gx', 'gy'), pairs + [(high, low) for low, high in p...  5.79 us
    ppermute x5, waiting for transfers between devices, swap(): lax.ppermute(value, ('gx', 'gy'), pairs + [(high, low) for low, high in p...  1.92 us
  transfers between devices with their start and end apart: 5, of which 1 were waited for; matrix products, arithmetic and copies ran while one was open for 0% of the time, Pallas kernels for 17%

profile of v4, /device:TPU:0, one launch (start us, length us, event | category | flops | bytes accessed | tf_op | source)
XLA Modules:
  0.0 14.1 jit_solution(5262455848142286430)
XLA Ops:
  0.0 2.2 %shard_map.82 = (bf16[4,16,48,128]{3,2,1,0:T(8,128)(2,1)S(1)}, f32[3,768,128]{2,1,0:T(8,128)S(1)}, f32[6,16,128]{2,1,0:T(8,128)S(1)}, f32[4,128]{1,0:T(4,128)S(1...) custom-call(f32[4]{0:T(128)} %visc_hbm.1, ...), custom_call_target="tpu_custom_call" | custom-call | flops 113246208 | bytes 1000000 | tf_op jit(solution)/shard_map/pallas_call | solution.py:711
  2.2 3.1 %collective-permute-start = (bf16[288,128]{1,0:T(8,128)(2,1)S(1)}, bf16[288,128]{1,0:T(8,128)(2,1)S(1)}, u32[]{:S(2)}, u32[]{:S(2)}) collective-permute-start(bf16[288,128]{1,0:T(8,128)(2,1)S(1)} %get-tuple-element.57), channel_id=1, source_target_pairs={{0,1},{4,5},{8,9},{12,13},{16,17},{20,21},{24,25},{28,29},{2,6},{1... | collective-permute-start | bytes 221192 | tf_op jit(solution)/shard_map/ppermute | solution.py:27
  5.3 0.0 collective-permute-start.1
  5.3 0.5 %collective-permute-start.2 = (bf16[288,128]{1,0:T(8,128)(2,1)S(1)}, bf16[288,128]{1,0:T(8,128)(2,1)S(1)}, u32[]{:S(2)}, u32[]{:S(2)}) collective-permute-start(bf16[288,128]{1,0:T(8,128)(2,1)S(1)} %get-tuple-element.59), channel_id=1, source_target_pairs={{2,3},{6,7},{10,11},{14,15},{18,19},{22,23},{26,27},{30,31},{0,4},... | collective-permute-start | bytes 221192 | tf_op jit(solution)/shard_map/ppermute | solution.py:27
  5.8 1.8 %shard_map.83 = (f32[6,16,48,128]{3,2,1,0:T(8,128)S(1)}, f32[2,5,8,128]{3,2,1,0:T(8,128)S(1)}, f32[2,16,128]{2,1,0:T(8,128)S(1)}, bf16[384,48]{1,0:T(8,128)(2,1)...) custom-call(bf16[4,16,48,128]{3,2,1,0:T(8,128)(2,1)S(1)} %get-tuple-element.41.l_ref, ...), custom_call_target="tpu_custom_call" | custom-call | flops 452984832 | bytes 1000000 | tf_op jit(solution)/shard_map/pallas_call | solution.py:711
  7.7 0.0 collective-permute-done.swap0_in
  7.7 0.0 collective-permute-done.1.swap1_in
  7.7 0.0 collective-permute-done.2.swap2_in
  7.7 0.3 %shard_map.84 = (f32[2,6,48,128]{3,2,1,0:T(8,128)S(1)}, f32[2,2,8,128]{3,2,1,0:T(8,128)S(1)}, f32[2,2,8,128]{3,2,1,0:T(8,128)S(1)}, f32[6,16,128]{2,1,0:T(8,128)...) custom-call(f32[4,128]{1,0:T(4,128)S(1)} %get-tuple-element.40.visc_, ...), custom_call_target="tpu_custom_call" | custom-call | flops 56623104 | bytes 1000000 | tf_op jit(solution)/shard_map/pallas_call | solution.py:711
  8.0 2.2 %collective-permute-start.3 = (bf16[336,128]{1,0:T(8,128)(2,1)S(1)}, bf16[336,128]{1,0:T(8,128)(2,1)S(1)}, u32[]{:S(2)}, u32[]{:S(2)}) collective-permute-start(bf16[336,128]{1,0:T(8,128)(2,1)S(1)} %get-tuple-element.72), channel_id=1, source_target_pairs={{4,8},{5,9},{6,10},{7,11},{12,16},{13,17},{14,18},{15,19},{20,24},... | collective-permute-start | bytes 258056 | tf_op jit(solution)/shard_map/ppermute | solution.py:27
  10.2 0.0 collective-permute-start.4
  10.2 0.5 %shard_map.85 = (f32[3,768,128]{2,1,0:T(8,128)S(1)}, f32[4,4,48,128]{3,2,1,0:T(8,128)S(1)}, f32[5,24,128]{2,1,0:T(8,128)S(1)}, f32[4,24,128]{2,1,0:T(8,128)S(1)}, f32[144,768]{1,0:T(8,128)S(1)}) custom-call(f32[4,128]{1,0:T(4,128)S(1)} %get-tuple-element.40.visc_ref, bf16[4,16,48,128]{3,2,1,0:T(8,128)(2,1)S(1)} %get-tuple-element.41.l_ref, ...), custom_call_target="tpu_custom_call" | custom-call | flops 113246208 | bytes 1000000 | tf_op jit(solution)/shard_map/pallas_call | solution.py:711
  10.8 1.9 %collective-permute-done.3.outer_in = bf16[336,128]{1,0:T(8,128)(2,1)S(1)} collective-permute-done((bf16[336,128]{1,0:T(8,128)(2,1)S(1)}, bf16[336,128]{1,0:T(8,128)(2,1)S(1)}, u32[]{:S(2)}, u32[]{:S(2)}) %collective-permute-start.3) | collective-permute-done | bytes 86048 | tf_op jit(solution)/shard_map/ppermute | solution.py:27
  12.7 0.0 collective-permute-done.4.inner_in
  12.7 1.4 %shard_map.86 = (bf16[3,768,128]{2,1,0:T(8,128)(2,1)}, f32[3,768,128]{2,1,0:T(8,128)S(1)}) custom-call(f32[4,128]{1,0:T(4,128)S(1)} %get-tuple-element.40.visc_ref, bf16[4,16,48,128]{3,2,1,0:T(8,128)(2,1)S(1)} %get-tuple-element.41.l_ref, f32[6,16,128]{2,1,0:T(8,128)S(1)} %get-tuple-element.42.kp_ref, ...), custom_call_target="tpu_custom_call", output_to_operand_aliasing={{1}: (6, {})} | custom-call | flops 169869312 | bytes 1000000 | tf_op jit(solution)/shard_map/pallas_call | solution.py:711
Async XLA Ops:
  2.2 5.5 %collective-permute-start = (bf16[288,128]{1,0:T(8,128)(2,1)S(1)}, bf16[288,128]{1,0:T(8,128)(2,1)S(1)}, u32[]{:S(2)}, u32[]{:S(2)}) collective-permute-start(bf16[288,128]{1,0:T(8,128)(2,1)S(1)} %get-tuple-element.57), channel_id=1, source_target_pairs={{0,1},{4,5},{8,9},{12,13},{16,17},{20,21},{24,25},{28,29},{2,6},{1... | collective-permute-start | bytes 221192 | tf_op jit(solution)/shard_map/ppermute | solution.py:27
  5.3 2.4 %collective-permute-start.1 = (bf16[288,128]{1,0:T(8,128)(2,1)S(1)}, bf16[288,128]{1,0:T(8,128)(2,1)S(1)}, u32[]{:S(2)}, u32[]{:S(2)}) collective-permute-start(bf16[288,128]{1,0:T(8,128)(2,1)S(1)} %get-tuple-element.58), channel_id=1, source_target_pairs={{1,2},{5,6},{9,10},{13,14},{17,18},{21,22},{25,26},{29,30},{0,4},{... | collective-permute-start | bytes 221192 | tf_op jit(solution)/shard_map/ppermute | solution.py:27
  5.3 2.4 %collective-permute-start.2 = (bf16[288,128]{1,0:T(8,128)(2,1)S(1)}, bf16[288,128]{1,0:T(8,128)(2,1)S(1)}, u32[]{:S(2)}, u32[]{:S(2)}) collective-permute-start(bf16[288,128]{1,0:T(8,128)(2,1)S(1)} %get-tuple-element.59), channel_id=1, source_target_pairs={{2,3},{6,7},{10,11},{14,15},{18,19},{22,23},{26,27},{30,31},{0,4},... | collective-permute-start | bytes 221192 | tf_op jit(solution)/shard_map/ppermute | solution.py:27
  8.0 4.6 %collective-permute-start.3 = (bf16[336,128]{1,0:T(8,128)(2,1)S(1)}, bf16[336,128]{1,0:T(8,128)(2,1)S(1)}, u32[]{:S(2)}, u32[]{:S(2)}) collective-permute-start(bf16[336,128]{1,0:T(8,128)(2,1)S(1)} %get-tuple-element.72), channel_id=1, source_target_pairs={{4,8},{5,9},{6,10},{7,11},{12,16},{13,17},{14,18},{15,19},{20,24},... | collective-permute-start | bytes 258056 | tf_op jit(solution)/shard_map/ppermute | solution.py:27
  10.2 2.5 %collective-permute-start.4 = (bf16[336,128]{1,0:T(8,128)(2,1)S(1)}, bf16[336,128]{1,0:T(8,128)(2,1)S(1)}, u32[]{:S(2)}, u32[]{:S(2)}) collective-permute-start(bf16[336,128]{1,0:T(8,128)(2,1)S(1)} %get-tuple-element.73), channel_id=1, source_target_pairs={{0,4},{1,5},{2,6},{3,7},{8,12},{9,13},{10,14},{11,15},{16,20},{17,... | collective-permute-start | bytes 258056 | tf_op jit(solution)/shard_map/ppermute | solution.py:27

commit v5 on v0

--- a/solution.py
+++ b/solution.py
@@ -406,32 +406,35 @@
                 v_ref[y - 1, i] = part
 
 
-def after_y(wx, wy, xs, visc_ref, l_ref, kp_ref, parts_ref, my_ref, own_ref, v3_ref, down_ref, up_ref):
-    z = l_ref.shape[3]
+def scales_top(wx, wy, x, kp_ref, misc_d):
+    row = lambda i, col: kp_ref[i, pl.ds(col, 1), :]
+    here = x * wy + wy - 1
+    visc = row(4, here)
+    scales = [
+        visc * row(0, here), visc if x == wx - 1 else visc * row(0, here + wy), visc * row(1, here),
+        visc * misc_d[x : x + 1], visc * row(2, here), visc * row(3, here),
+    ]
+    return visc, scales
+
+
+def y_vertex(wx, wy, xs, visc_ref, kp_ref, parts_ref, my_ref, own_ref, v3_ref, down_ref, up_ref):
+    z = kp_ref.shape[2]
     misc_d = read_tail(down_ref, wx, 0)[2]
     misc_u = read_tail(up_ref, wx, 1)[2]
     row = lambda i, col: kp_ref[i, pl.ds(col, 1), :]
-    delta = dot(my_ref[...], wide([down_ref[pl.ds(48 * x, 48), :] for x in xs]))
-    arrived = [up_ref[pl.ds(48 * x, 48), :].astype(F32) for x in xs]
-    arrived_corners = slot_corners(arrived, parts_ref, 3)
+    delta = dot(my_ref[pl.ds(288, 96), :], wide([down_ref[pl.ds(48 * x, 48), :] for x in xs]))
+    arrived_corners = slot_corners([up_ref[pl.ds(48 * x, 48), :] for x in xs], parts_ref, 3)
     results = []
     for n, x in enumerate(xs):
-        here = x * wy + wy - 1
         last = x == wx - 1
         part = delta[:, z * n : z * n + z]
-        visc = row(4, here)
-        scales = [
-            visc * row(0, here), visc if last else visc * row(0, here + wy), visc * row(1, here),
-            visc * misc_d[x : x + 1], visc * row(2, here), visc * row(3, here),
-        ]
-        flux = [part[48 * s : 48 * s + 48] * scales[s] for s in range(6)]
+        visc, scales = scales_top(wx, wy, x, kp_ref, misc_d)
         used = [None if (s == 1 and last) else scales[s] for s in range(6)]
         known = v3_ref[x] * misc_d[x : x + 1]
-        top = [rows + settle(known, p) for p, rows in enumerate(scaled_corners(part[288:384], used))]
-        top_one = part[304:320] * visc
-        here = x * wy
+        top = [rows + settle(known, p) for p, rows in enumerate(scaled_corners(part, used))]
+        top_one = part[16:32] * visc
         visc = level_visc(misc_u[x : x + 1], visc_ref)
-        flag = row(1, here)
+        flag = row(1, x * wy)
         own = own_ref[:, pl.ds(z * x, z)]
         keep_z = misc_u[2 * wx + x : 2 * wx + x + 1]
         scales = [
@@ -440,33 +443,43 @@
         ]
         known = arrived_corners[n] * flag
         low = [rows + settle(known, p) for p, rows in enumerate(scaled_corners(own[48:144], scales))]
-        low_one = own[64:80] * visc
-        face = (arrived[n] + visc * (own[0:48] + penalty * l_ref[1, here].astype(F32))) * flag
-        results.append((flux, top, top_one, low, low_one, face))
+        results.append((top, low, top_one, own[64:80] * visc))
+    return results
+
+
+def y_flux(wx, wy, visc_ref, l_ref, kp_ref, my_ref, own_ref, down_ref, up_ref):
+    misc_d = read_tail(down_ref, wx, 0)[2]
+    misc_u = read_tail(up_ref, wx, 1)[2]
+    delta = columns(dot(my_ref[pl.ds(0, 288), :], wide([down_ref[pl.ds(48 * x, 48), :] for x in range(wx)])), wx)
+    own = columns(own_ref[0:48, :], wx)
+    results = []
+    for x in range(wx):
+        scales = scales_top(wx, wy, x, kp_ref, misc_d)[1]
+        flux = [delta[x][48 * s : 48 * s + 48] * scales[s] for s in range(6)]
+        visc = level_visc(misc_u[x : x + 1], visc_ref)
+        arrived = up_ref[pl.ds(48 * x, 48), :].astype(F32)
+        face = arrived + visc * (own[x] + penalty * l_ref[1, x * wy].astype(F32))
+        results.append((flux, face * kp_ref[1, pl.ds(x * wy, 1), :]))
     return results
 
 
 def turn_kernel(
     wx, wy, visc_ref, l_ref, kp_ref, diag_ref, parts_ref, my_ref, own_ref, c_ref, va_ref, vb_ref,
     v1a_ref, v1b_ref, v3_ref, swap0_in, swap1_in, swap2_in,
-    c3_ref, vt_ref, vl_ref, v1_ref, face_ref, yd_ref, yu_ref, inner_ref, outer_ref, down_ref, up_ref,
+    vt_ref, vl_ref, v1_ref, yd_ref, yu_ref, inner_ref, outer_ref, down_ref, up_ref,
 ):
     z = l_ref.shape[3]
     arrive((swap0_in, swap1_in, swap2_in), yd_ref, yu_ref)
     xs = (0, wx - 1)
-    results = after_y(wx, wy, xs, visc_ref, l_ref, kp_ref, parts_ref, my_ref, own_ref, v3_ref, yd_ref, yu_ref)
-    row = lambda i, col: kp_ref[i, pl.ds(col, 1), :]
+    results = y_vertex(wx, wy, xs, visc_ref, kp_ref, parts_ref, my_ref, own_ref, v3_ref, yd_ref, yu_ref)
     sums_d, one_d, misc_d = read_tail(yd_ref, wx, 0)
     sums_u, one_u, misc_u = read_tail(yu_ref, wx, 1)
     edge_high, edge_low = misc_d[wx + 4 : 2 * wx + 4], misc_d[2 * wx + 4 : 3 * wx + 4]
-    for n, (flux, top, top_one, low, low_one, face) in enumerate(results):
-        for s in range(6):
-            c3_ref[n, s] = flux[s]
-        face_ref[n] = face
+    for n, (top, low, _, _) in enumerate(results):
         for p in range(2):
             vt_ref[n, p] = top[p]
             vl_ref[n, p] = low[p]
-    flux, top, top_one, low, low_one, face = results[1]
+    top_one, low_one = results[1][2:]
     mine = tall(one_u) + low_one
     v1_ref[0] = mine
     v1_ref[1] = v1a_ref[0]
@@ -491,9 +504,11 @@
     rim += [misc_u[wx : wx + 1], kp_ref[0, 0:wy], misc_d[wx : wx + 1]]
     put_tail(down_ref, 48 * (wy + 2), rim)
     corner = (wx - 1) * wy
+    last_trace = yd_ref[pl.ds(48 * (wx - 1), 48), :]
+    flux = dot(my_ref[pl.ds(48, 48), :], last_trace) * kp_ref[4, pl.ds(corner + wy - 1, 1), :]
     for y in range(wy):
         part = c_ref[1, corner + y]
-        up_ref[pl.ds(48 * y, 48), :] = (part + flux[1] if y == wy - 1 else part).astype(BF)
+        up_ref[pl.ds(48 * y, 48), :] = (part + flux if y == wy - 1 else part).astype(BF)
     last = pl.ds(corner, wy)
     rim = [plane(wx, 1, 1), mine, *one_d]
     rim += [misc_u[wx - 1 : wx], kp_ref[5, last], misc_d[wx + 1 : wx + 2]]
@@ -504,17 +519,19 @@
 
 
 def assemble_kernel(
-    wx, wy, visc_ref, l_ref, kp_ref, diag_ref, parts_ref, mx_ref, my_ref, own_ref, c_ref, c3_ref,
-    va_ref, vb_ref, v3_ref, vt_ref, vl_ref, face_ref, yd_ref, yu_ref,
+    wx, wy, visc_ref, l_ref, kp_ref, diag_ref, parts_ref, mx_ref, my_ref, own_ref, c_ref,
+    va_ref, vb_ref, v3_ref, vt_ref, vl_ref, yd_ref, yu_ref,
     r_ref, late_ref, v_ref, inv_ref, ownx_ref, mid,
 ):
     z = l_ref.shape[3]
     cells = wx * wy
     xs = tuple(range(1, wx - 1))
-    results = after_y(wx, wy, xs, visc_ref, l_ref, kp_ref, parts_ref, my_ref, own_ref, v3_ref, yd_ref, yu_ref)
-    for n, part in enumerate(results):
+    results = y_vertex(wx, wy, xs, visc_ref, kp_ref, parts_ref, my_ref, own_ref, v3_ref, yd_ref, yu_ref)
+    faces = []
+    for x, (flux, face) in enumerate(y_flux(wx, wy, visc_ref, l_ref, kp_ref, my_ref, own_ref, yd_ref, yu_ref)):
+        faces.append(face)
         for s in range(6):
-            mid[n, s] = part[0][s]
+            mid[x, s] = flux[s]
     traces = [yu_ref[pl.ds(48 * wx, 48), :]] + [l_ref[0, y] for y in range(wy)] + [yd_ref[pl.ds(48 * wx, 48), :]]
     ownx_ref[...] = dot(mx_ref[pl.ds(240, 144), :], wide(traces))
 
@@ -522,17 +539,12 @@
         here = c_ref[slot, x * wy + y]
         if y < wy - 1:
             return here
-        return here + (mid[x - 1, slot] if 0 < x < wx - 1 else c3_ref[0 if x == 0 else 1, slot])
+        return here + mid[x, slot]
 
     for x in range(wx):
         for y in range(wy):
             col = pl.ds(x * wy + y, 48, stride=cells)
-            if y:
-                behind = contrib(3, x, y - 1)
-            elif 0 < x < wx - 1:
-                behind = results[x - 1][5]
-            else:
-                behind = face_ref[0 if x == 0 else 1]
+            behind = contrib(3, x, y - 1) if y else faces[x]
             ahead = contrib(0, x, y) + contrib(1, x - 1, y) if x else contrib(0, x, y)
             sides = [ahead, contrib(2, x, y) + behind, contrib(4, x, y) + z_prev(contrib(5, x, y))]
             for d in range(3):
@@ -547,7 +559,7 @@
     edge_diag = misc_d[wx + 4 : 2 * wx + 4] + misc_d[2 * wx + 4 : 3 * wx + 4]
 
     def brought(which, i):
-        held = vt_ref if which == 1 else vl_ref
+        held = vl_ref if which else vt_ref
         terms = []
         for x, p in ((i, 0), (i - 1, 1)):
             if x in (0, wx - 1):
@@ -557,9 +569,9 @@
         return sum(terms[1:], terms[0])
 
     for i in range(wx + 1):
-        lines = [sums_u[i] + brought(3, i), va_ref[0, i]]
+        lines = [sums_u[i] + brought(1, i), va_ref[0, i]]
         lines += [vb_ref[y, i] for y in range(wy - 2)]
-        lines += [va_ref[1, i] + brought(1, i), sums_d[i]]
+        lines += [va_ref[1, i] + brought(0, i), sums_d[i]]
         v_ref[i] = merge(lines[1::2], lines[0::2])
         if i < wx:
             parts = [jnp.broadcast_to(diag_ref[pl.ds(i * wy + y, 1), :], (4, z)) for y in range(wy)]
@@ -692,9 +704,8 @@
                 for b, value in enumerate(between(lines[0][a], lines[1][a])):
                     at = pl.ds(cells * (16 * c + 4 * a + b), cells)
                     held[d, at, :] = (r_ref[d, at, :] + value).astype(BF)
-            part = pl.ds(16 * cells * c, 16 * cells)
-            copies.append(pltpu.make_async_copy(held.at[d, part], out_hbm.at[d, part], sems.at[3 * d + c]))
-            copies[-1].start()
+        copies.append(pltpu.make_async_copy(held.at[d], out_hbm.at[d], sems.at[d]))
+        copies[d].start()
     for copy in copies:
         copy.wait()
 
@@ -757,14 +768,14 @@
         ),
         [vm((4, cells, 48, z), BF), vm((384, 288), BF), vm((288, 256), BF)], cells * per_hex,
     )
-    c3, vt, vl, v1, face, yd, yu, inner, outer = call(
+    vt, vl, v1, yd, yu, inner, outer = call(
         bind(turn_kernel),
         (
             visc, lifted, flags, diag, parts, my, own, c, va, vb, v1a, v1b, v3, *swaps,
         ),
         (
-            vm((2, 6, 48, z), F32), vm((2, 2, 8, z), F32), vm((2, 2, 8, z), F32), vm((wy + 2, 16, z), F32),
-            vm((2, 48, z), F32), y_message, y_message, x_message, x_message,
+            vm((2, 2, 8, z), F32), vm((2, 2, 8, z), F32), vm((wy + 2, 16, z), F32),
+            y_message, y_message, x_message, x_message,
         ),
         [x_message, x_message], 2 * per_hex,
     )
@@ -773,13 +784,13 @@
     residual, late, vs, inverse, ownx = call(
         bind(assemble_kernel),
         (
-            visc, lifted, flags, diag, parts, mx, my, own, c, c3, va, vb, v3, vt, vl, face, yd, yu,
+            visc, lifted, flags, diag, parts, mx, my, own, c, va, vb, v3, vt, vl, yd, yu,
         ),
         (
             vm((3, 48 * cells, z), F32), vm((4, wy, 48, z), F32), vm((wx + 1, rows, z), F32), vm((wx, rows, z), F32),
             vm((144, (wy + 2) * z), F32),
         ),
-        [vm((wx - 2, 6, 48, z), F32)], 4 * per_hex,
+        [vm((wx, 6, 48, z), F32)], 4 * per_hex,
     )
     out, _ = call(
         bind(final_kernel),
@@ -787,7 +798,7 @@
             visc, lifted, flags, parts, mx, ownx, residual, late, vs, inverse, v1, yd, yu, outer, inner,
         ),
         (jax.ShapeDtypeStruct((3, 48 * cells, z), BF), vm((3, 48 * cells, z), F32)),
-        [vm((3, 48 * cells, z), BF), vm((2, 4 * wy * (wx + 1), z), F32), pltpu.SemaphoreType.DMA((9,))], 6 * per_hex,
+        [vm((3, 48 * cells, z), BF), vm((2, 4 * wy * (wx + 1), z), F32), pltpu.SemaphoreType.DMA((3,))], 6 * per_hex,
         aliases={6: 1},
     )
     return out.reshape(traces.shape)

time: 14.3 us -> 14.2 us (level)
  no operation moved by 1% of the time
where the time goes in v5:
time: 14.2 us; the launch traced here: 14 us
  Pallas kernels  6.26 us (44%)
  starting transfers between devices  5.75 us (40%)
  waiting for transfers between devices  1.9 us (13%)
    pallas_call x5, Pallas kernels, call(): pl.pallas_call(body, **keywords, in_specs=[pl.BlockSpec(memory_space=pltp...  6.26 us
    ppermute x5, starting transfers between devices, swap(): lax.ppermute(value, ('gx', 'gy'), pairs + [(high, low) for low, high in p...  5.75 us
    ppermute x5, waiting for transfers between devices, swap(): lax.ppermute(value, ('gx', 'gy'), pairs + [(high, low) for low, high in p...  1.9 us
  transfers between devices with their start and end apart: 5, of which 1 were waited for; matrix products, arithmetic and copies ran while one was open for 0% of the time, Pallas kernels for 17%

profile of v5, /device:TPU:0, one launch (start us, length us, event | category | flops | bytes accessed | tf_op | source)
XLA Modules:
  0.0 14.0 jit_solution(7125988830564274952)
XLA Ops:
  0.0 2.2 %shard_map.82 = (bf16[4,16,48,128]{3,2,1,0:T(8,128)(2,1)S(1)}, f32[3,768,128]{2,1,0:T(8,128)S(1)}, f32[6,16,128]{2,1,0:T(8,128)S(1)}, f32[4,128]{1,0:T(4,128)S(1...) custom-call(f32[4]{0:T(128)} %visc_hbm.1, ...), custom_call_target="tpu_custom_call" | custom-call | flops 113246208 | bytes 1000000 | tf_op jit(solution)/shard_map/pallas_call | solution.py:720
  2.2 3.1 %collective-permute-start = (bf16[288,128]{1,0:T(8,128)(2,1)S(1)}, bf16[288,128]{1,0:T(8,128)(2,1)S(1)}, u32[]{:S(2)}, u32[]{:S(2)}) collective-permute-start(bf16[288,128]{1,0:T(8,128)(2,1)S(1)} %get-tuple-element.55), channel_id=1, source_target_pairs={{0,1},{4,5},{8,9},{12,13},{16,17},{20,21},{24,25},{28,29},{2,6},{1... | collective-permute-start | bytes 221192 | tf_op jit(solution)/shard_map/ppermute | solution.py:27
  5.3 0.0 collective-permute-start.1
  5.3 0.5 %collective-permute-start.2 = (bf16[288,128]{1,0:T(8,128)(2,1)S(1)}, bf16[288,128]{1,0:T(8,128)(2,1)S(1)}, u32[]{:S(2)}, u32[]{:S(2)}) collective-permute-start(bf16[288,128]{1,0:T(8,128)(2,1)S(1)} %get-tuple-element.57), channel_id=1, source_target_pairs={{2,3},{6,7},{10,11},{14,15},{18,19},{22,23},{26,27},{30,31},{0,4},... | collective-permute-start | bytes 221192 | tf_op jit(solution)/shard_map/ppermute | solution.py:27
  5.8 1.9 %shard_map.83 = (f32[6,16,48,128]{3,2,1,0:T(8,128)S(1)}, f32[2,5,8,128]{3,2,1,0:T(8,128)S(1)}, f32[2,16,128]{2,1,0:T(8,128)S(1)}, bf16[384,48]{1,0:T(8,128)(2,1)...) custom-call(bf16[4,16,48,128]{3,2,1,0:T(8,128)(2,1)S(1)} %get-tuple-element.39.l_ref, ...), custom_call_target="tpu_custom_call" | custom-call | flops 452984832 | bytes 1000000 | tf_op jit(solution)/shard_map/pallas_call | solution.py:720
  7.6 0.0 collective-permute-done.swap0_in
  7.6 0.0 collective-permute-done.1.swap1_in
  7.7 0.0 collective-permute-done.2.swap2_in
  7.7 0.3 %shard_map.84 = (f32[2,2,8,128]{3,2,1,0:T(8,128)S(1)}, f32[2,2,8,128]{3,2,1,0:T(8,128)S(1)}, f32[6,16,128]{2,1,0:T(8,128)S(1)}, bf16[288,128]{1,0:T(8,128)(2,1)S...) custom-call(f32[4,128]{1,0:T(4,128)S(1)} %get-tuple-element.38.visc_ref, ...), custom_call_target="tpu_custom_call" | custom-call | flops 56623104 | bytes 1000000 | tf_op jit(solution)/shard_map/pallas_call | solution.py:720
  8.0 2.2 %collective-permute-start.3 = (bf16[336,128]{1,0:T(8,128)(2,1)S(1)}, bf16[336,128]{1,0:T(8,128)(2,1)S(1)}, u32[]{:S(2)}, u32[]{:S(2)}) collective-permute-start(bf16[336,128]{1,0:T(8,128)(2,1)S(1)} %get-tuple-element.68), channel_id=1, source_target_pairs={{4,8},{5,9},{6,10},{7,11},{12,16},{13,17},{14,18},{15,19},{20,24},... | collective-permute-start | bytes 258056 | tf_op jit(solution)/shard_map/ppermute | solution.py:27
  10.1 0.0 collective-permute-start.4
  10.1 0.6 %shard_map.85 = (f32[3,768,128]{2,1,0:T(8,128)S(1)}, f32[4,4,48,128]{3,2,1,0:T(8,128)S(1)}, f32[5,24,128]{2,1,0:T(8,128)S(1)}, f32[4,24,128]{2,1,0:T(8,128)S(1)}, f32[144,768]{1,0:T(8,128)S(1)}) custom-call(f32[4,128]{1,0:T(4,128)S(1)} %get-tuple-element.38.visc_ref, bf16[4,16,48,128]{3,2,1,0:T(8,128)(2,1)S(1)} %get-tuple-element.39.l_ref, ...), custom_call_target="tpu_custom_call" | custom-call | flops 113246208 | bytes 1000000 | tf_op jit(solution)/shard_map/pallas_call | solution.py:720
  10.7 1.9 %collective-permute-done.3.outer_in = bf16[336,128]{1,0:T(8,128)(2,1)S(1)} collective-permute-done((bf16[336,128]{1,0:T(8,128)(2,1)S(1)}, bf16[336,128]{1,0:T(8,128)(2,1)S(1)}, u32[]{:S(2)}, u32[]{:S(2)}) %collective-permute-start.3) | collective-permute-done | bytes 86048 | tf_op jit(solution)/shard_map/ppermute | solution.py:27
  12.6 0.0 collective-permute-done.4.inner_in
  12.6 1.4 %shard_map.86 = (bf16[3,768,128]{2,1,0:T(8,128)(2,1)}, f32[3,768,128]{2,1,0:T(8,128)S(1)}) custom-call(f32[4,128]{1,0:T(4,128)S(1)} %get-tuple-element.38.visc_ref, bf16[4,16,48,128]{3,2,1,0:T(8,128)(2,1)S(1)} %get-tuple-element.39.l_ref, f32[6,16,128]{2,1,0:T(8,128)S(1)} %get-tuple-element.40.kp_ref, ...), custom_call_target="tpu_custom_call", output_to_operand_aliasing={{1}: (6, {})} | custom-call | flops 169869312 | bytes 1000000 | tf_op jit(solution)/shard_map/pallas_call | solution.py:720
Async XLA Ops:
  2.2 5.5 %collective-permute-start = (bf16[288,128]{1,0:T(8,128)(2,1)S(1)}, bf16[288,128]{1,0:T(8,128)(2,1)S(1)}, u32[]{:S(2)}, u32[]{:S(2)}) collective-permute-start(bf16[288,128]{1,0:T(8,128)(2,1)S(1)} %get-tuple-element.55), channel_id=1, source_target_pairs={{0,1},{4,5},{8,9},{12,13},{16,17},{20,21},{24,25},{28,29},{2,6},{1... | collective-permute-start | bytes 221192 | tf_op jit(solution)/shard_map/ppermute | solution.py:27
  5.3 2.4 %collective-permute-start.1 = (bf16[288,128]{1,0:T(8,128)(2,1)S(1)}, bf16[288,128]{1,0:T(8,128)(2,1)S(1)}, u32[]{:S(2)}, u32[]{:S(2)}) collective-permute-start(bf16[288,128]{1,0:T(8,128)(2,1)S(1)} %get-tuple-element.56), channel_id=1, source_target_pairs={{1,2},{5,6},{9,10},{13,14},{17,18},{21,22},{25,26},{29,30},{0,4},{... | collective-permute-start | bytes 221192 | tf_op jit(solution)/shard_map/ppermute | solution.py:27
  5.3 2.4 %collective-permute-start.2 = (bf16[288,128]{1,0:T(8,128)(2,1)S(1)}, bf16[288,128]{1,0:T(8,128)(2,1)S(1)}, u32[]{:S(2)}, u32[]{:S(2)}) collective-permute-start(bf16[288,128]{1,0:T(8,128)(2,1)S(1)} %get-tuple-element.57), channel_id=1, source_target_pairs={{2,3},{6,7},{10,11},{14,15},{18,19},{22,23},{26,27},{30,31},{0,4},... | collective-permute-start | bytes 221192 | tf_op jit(solution)/shard_map/ppermute | solution.py:27
  8.0 4.6 %collective-permute-start.3 = (bf16[336,128]{1,0:T(8,128)(2,1)S(1)}, bf16[336,128]{1,0:T(8,128)(2,1)S(1)}, u32[]{:S(2)}, u32[]{:S(2)}) collective-permute-start(bf16[336,128]{1,0:T(8,128)(2,1)S(1)} %get-tuple-element.68), channel_id=1, source_target_pairs={{4,8},{5,9},{6,10},{7,11},{12,16},{13,17},{14,18},{15,19},{20,24},... | collective-permute-start | bytes 258056 | tf_op jit(solution)/shard_map/ppermute | solution.py:27
  10.1 2.5 %collective-permute-start.4 = (bf16[336,128]{1,0:T(8,128)(2,1)S(1)}, bf16[336,128]{1,0:T(8,128)(2,1)S(1)}, u32[]{:S(2)}, u32[]{:S(2)}) collective-permute-start(bf16[336,128]{1,0:T(8,128)(2,1)S(1)} %get-tuple-element.69), channel_id=1, source_target_pairs={{0,4},{1,5},{2,6},{3,7},{8,12},{9,13},{10,14},{11,15},{16,20},{17,... | collective-permute-start | bytes 258056 | tf_op jit(solution)/shard_map/ppermute | solution.py:27

commit v6 on v5

--- a/solution.py
+++ b/solution.py
@@ -205,7 +205,7 @@
 
 def first_kernel(
     wx, wy, visc_hbm, t_hbm, dir_hbm, cls_hbm, diag_hbm, st_hbm, f_hbm, parts_hbm,
-    l_ref, nat, kp_ref, visc_ref, diag_ref, st_ref, f_ref, parts_ref, v_ref, v1_ref, v3_ref,
+    l_ref, nat, kp_ref, visc_ref, diag_ref, st_ref, f_ref, parts_ref, made_ref, v_ref, v1_ref, v3_ref,
     swap0_ref, swap1_ref, swap2_ref, down_ref, up_ref, t_ref, dir_ref, cls_ref, levels, sems,
 ):
     cells = wx * wy
@@ -273,6 +273,10 @@
     put_tail(up_ref, 48 * wx + 48, rim)
     depart_three(down_ref, up_ref, (swap0_ref, swap1_ref, swap2_ref))
 
+    @pl.when(jnp.logical_not(even("gx")))
+    def _():
+        face_matrix(1, made_ref, st_ref, f_ref, parts_ref)
+
 
 def tail_rows(count):
     return -(-count // 16) * 16
@@ -369,15 +373,27 @@
     ]
 
 
+def face_matrix(slot, ref, st_ref, f_ref, parts_ref):
+    bare, flux = product(f_ref, st_ref, slot)
+    turned = tall([bare[0:48], bare[96:288], bare[48:96]]) if slot == 1 else bare
+    ref[pl.ds(0, 288), :] = turned.astype(BF)
+    ref[pl.ds(288, 96), :] = vertex_part(flux, parts_ref).astype(BF)
+
+
 def middle_kernel(
-    wx, wy, l_ref, nat, kp_ref, st_ref, f_ref, parts_ref,
+    wx, wy, l_ref, nat, kp_ref, st_ref, f_ref, parts_ref, made_ref,
     c_ref, v_ref, v1_ref, mx_ref, my_ref, own_ref, rest_ref, m_ref, lost_ref,
 ):
-    for slot, ref in ((1, mx_ref), (3, my_ref)):
-        bare, flux = product(f_ref, st_ref, slot)
-        turned = tall([bare[0:48], bare[96:288], bare[48:96]]) if slot == 1 else bare
-        ref[pl.ds(0, 288), :] = turned.astype(BF)
-        ref[pl.ds(288, 96), :] = vertex_part(flux, parts_ref).astype(BF)
+    face_matrix(3, my_ref, st_ref, f_ref, parts_ref)
+
+    @pl.when(even("gx"))
+    def _():
+        face_matrix(1, mx_ref, st_ref, f_ref, parts_ref)
+
+    @pl.when(jnp.logical_not(even("gx")))
+    def _():
+        mx_ref[...] = made_ref[...]
+
     flux = product(f_ref, st_ref, None)[1]
     m_ref[pl.ds(0, 288), :] = flux.astype(BF)
     m_ref[pl.ds(288, 96), :] = vertex_part(flux, parts_ref).astype(BF)
@@ -739,7 +755,7 @@
     y_message = vm((48 * wx + 48 + tail_rows(8 * ((wx + 2) // 2) + 8 + 3 * wx + 4), z), BF)
     x_message = vm((48 * (wy + 2) + tail_rows(rows + 3 * wy + 4), z), BF)
 
-    (lifted, nat, flags, visc, diag, s_turned, f_map, parts, va, v1a, v3, *swaps) = call(
+    (lifted, nat, flags, visc, diag, s_turned, f_map, parts, made, va, v1a, v3, *swaps) = call(
         bind(first_kernel),
         (
             viscosity, traces.reshape(3, 48 * cells, z), dirichlet.reshape(3, cells, z),
@@ -747,7 +763,7 @@
         ),
         (
             vm((4, cells, 48, z), BF), vm((3, 48 * cells, z), F32), vm((6, cells, z), F32), vm((viscosity.shape[0], z), F32), vm((cells, z), F32),
-            vm(solve_map.shape[::-1], BF), vm(flux_map.shape, BF), vm(parts.shape, BF),
+            vm(solve_map.shape[::-1], BF), vm(flux_map.shape, BF), vm(parts.shape, BF), vm((384, 48), BF),
             vm((2, wx + 1, 8, z), F32), vm((2, 16, z), F32), vm((wx, 32, z), F32),
             y_message, y_message, y_message,
         ),
@@ -761,7 +777,7 @@
     swaps = [swap(message, "gy", "gx", k, 3) for k, message in enumerate(swaps)]
     c, vb, v1b, mx, my, own = call(
         bind(middle_kernel),
-        (lifted, nat, flags, s_turned, f_map, parts),
+        (lifted, nat, flags, s_turned, f_map, parts, made),
         (
             vm((6, cells, 48, z), F32), vm((wy - 2, wx + 1, 8, z), F32), vm((wy - 2, 16, z), F32),
             vm((384, 48), BF), vm((384, 48), BF), vm((144, wx * z), F32),

time: 14.2 us -> 14.3 us (level)
  starting transfers between devices: 5.75 us -> 5.5 us
  Pallas kernels: 6.26 us -> 6.49 us
  waiting for transfers between devices: 1.9 us -> 2.07 us
    ppermute x5, starting transfers between devices: 5.75 us -> 5.5 us  [swap(): lax.ppermute(value, ('gx', 'gy'), pairs + [(high, low) for low, high in p...]
    pallas_call x5, Pallas kernels: 6.26 us -> 6.49 us  [call(): pl.pallas_call(body, **keywords, in_specs=[pl.BlockSpec(memory_space=pltp...]
    ppermute x5, waiting for transfers between devices: 1.9 us -> 2.07 us  [swap(): lax.ppermute(value, ('gx', 'gy'), pairs + [(high, low) for low, high in p...]
  transfers between devices with their start and end apart: 5 -> 5, of which waited for: 1 -> 1; matrix products, arithmetic and copies ran while one was open for 0% -> 0% of each run, Pallas kernels for 17% -> 19%
where the time goes in v6:
time: 14.3 us; the launch traced here: 14.1 us
  Pallas kernels  6.49 us (45%)
  starting transfers between devices  5.5 us (38%)
  waiting for transfers between devices  2.07 us (14%)
    pallas_call x5, Pallas kernels, call(): pl.pallas_call(body, **keywords, in_specs=[pl.BlockSpec(memory_space=pltp...  6.49 us
    ppermute x5, starting transfers between devices, swap(): lax.ppermute(value, ('gx', 'gy'), pairs + [(high, low) for low, high in p...  5.5 us
    ppermute x5, waiting for transfers between devices, swap(): lax.ppermute(value, ('gx', 'gy'), pairs + [(high, low) for low, high in p...  2.07 us
  transfers between devices with their start and end apart: 5, of which 1 were waited for; matrix products, arithmetic and copies ran while one was open for 0% of the time, Pallas kernels for 19%

profile of v6, /device:TPU:0, one launch (start us, length us, event | category | flops | bytes accessed | tf_op | source)
XLA Modules:
  0.0 14.1 jit_solution(17954690248418357629)
XLA Ops:
  0.0 2.2 %shard_map.82 = (bf16[4,16,48,128]{3,2,1,0:T(8,128)(2,1)S(1)}, f32[3,768,128]{2,1,0:T(8,128)S(1)}, f32[6,16,128]{2,1,0:T(8,128)S(1)}, f32[4,128]{1,0:T(4,128)S(1...) custom-call(f32[4]{0:T(128)} %visc_hbm.1, ...), custom_call_target="tpu_custom_call" | custom-call | flops 113246208 | bytes 1000000 | tf_op jit(solution)/shard_map/pallas_call | solution.py:736
  2.2 3.1 %collective-permute-start = (bf16[288,128]{1,0:T(8,128)(2,1)S(1)}, bf16[288,128]{1,0:T(8,128)(2,1)S(1)}, u32[]{:S(2)}, u32[]{:S(2)}) collective-permute-start(bf16[288,128]{1,0:T(8,128)(2,1)S(1)} %get-tuple-element.57), channel_id=1, source_target_pairs={{0,1},{4,5},{8,9},{12,13},{16,17},{20,21},{24,25},{28,29},{2,6},{1... | collective-permute-start | bytes 221192 | tf_op jit(solution)/shard_map/ppermute | solution.py:27
  5.2 0.0 collective-permute-start.1
  5.2 0.5 %collective-permute-start.2 = (bf16[288,128]{1,0:T(8,128)(2,1)S(1)}, bf16[288,128]{1,0:T(8,128)(2,1)S(1)}, u32[]{:S(2)}, u32[]{:S(2)}) collective-permute-start(bf16[288,128]{1,0:T(8,128)(2,1)S(1)} %get-tuple-element.59), channel_id=1, source_target_pairs={{2,3},{6,7},{10,11},{14,15},{18,19},{22,23},{26,27},{30,31},{0,4},... | collective-permute-start | bytes 221192 | tf_op jit(solution)/shard_map/ppermute | solution.py:27
  5.8 2.1 %shard_map.83 = (f32[6,16,48,128]{3,2,1,0:T(8,128)S(1)}, f32[2,5,8,128]{3,2,1,0:T(8,128)S(1)}, f32[2,16,128]{2,1,0:T(8,128)S(1)}, bf16[384,48]{1,0:T(8,128)(2,1)...) custom-call(bf16[4,16,48,128]{3,2,1,0:T(8,128)(2,1)S(1)} %get-tuple-element.40.l_ref, ...), custom_call_target="tpu_custom_call" | custom-call | flops 452984832 | bytes 1000000 | tf_op jit(solution)/shard_map/pallas_call | solution.py:736
  7.9 0.0 collective-permute-done.swap0_in
  7.9 0.0 collective-permute-done.1.swap1_in
  7.9 0.0 collective-permute-done.2.swap2_in
  7.9 0.3 %shard_map.84 = (f32[2,2,8,128]{3,2,1,0:T(8,128)S(1)}, f32[2,2,8,128]{3,2,1,0:T(8,128)S(1)}, f32[6,16,128]{2,1,0:T(8,128)S(1)}, bf16[288,128]{1,0:T(8,128)(2,1)S...) custom-call(f32[4,128]{1,0:T(4,128)S(1)} %get-tuple-element.39.visc_ref, ...), custom_call_target="tpu_custom_call" | custom-call | flops 56623104 | bytes 1000000 | tf_op jit(solution)/shard_map/pallas_call | solution.py:736
  8.2 1.9 %collective-permute-start.3 = (bf16[336,128]{1,0:T(8,128)(2,1)S(1)}, bf16[336,128]{1,0:T(8,128)(2,1)S(1)}, u32[]{:S(2)}, u32[]{:S(2)}) collective-permute-start(bf16[336,128]{1,0:T(8,128)(2,1)S(1)} %get-tuple-element.70), channel_id=1, source_target_pairs={{4,8},{5,9},{6,10},{7,11},{12,16},{13,17},{14,18},{15,19},{20,24},... | collective-permute-start | bytes 258056 | tf_op jit(solution)/shard_map/ppermute | solution.py:27
  10.1 0.0 collective-permute-start.4
  10.1 0.6 %shard_map.85 = (f32[3,768,128]{2,1,0:T(8,128)S(1)}, f32[4,4,48,128]{3,2,1,0:T(8,128)S(1)}, f32[5,24,128]{2,1,0:T(8,128)S(1)}, f32[4,24,128]{2,1,0:T(8,128)S(1)}, f32[144,768]{1,0:T(8,128)S(1)}) custom-call(f32[4,128]{1,0:T(4,128)S(1)} %get-tuple-element.39.visc_ref, bf16[4,16,48,128]{3,2,1,0:T(8,128)(2,1)S(1)} %get-tuple-element.40.l_ref, ...), custom_call_target="tpu_custom_call" | custom-call | flops 113246208 | bytes 1000000 | tf_op jit(solution)/shard_map/pallas_call | solution.py:736
  10.7 2.1 %collective-permute-done.3.outer_in = bf16[336,128]{1,0:T(8,128)(2,1)S(1)} collective-permute-done((bf16[336,128]{1,0:T(8,128)(2,1)S(1)}, bf16[336,128]{1,0:T(8,128)(2,1)S(1)}, u32[]{:S(2)}, u32[]{:S(2)}) %collective-permute-start.3) | collective-permute-done | bytes 86048 | tf_op jit(solution)/shard_map/ppermute | solution.py:27
  12.8 0.0 collective-permute-done.4.inner_in
  12.8 1.4 %shard_map.86 = (bf16[3,768,128]{2,1,0:T(8,128)(2,1)}, f32[3,768,128]{2,1,0:T(8,128)S(1)}) custom-call(f32[4,128]{1,0:T(4,128)S(1)} %get-tuple-element.39.visc_ref, bf16[4,16,48,128]{3,2,1,0:T(8,128)(2,1)S(1)} %get-tuple-element.40.l_ref, f32[6,16,128]{2,1,0:T(8,128)S(1)} %get-tuple-element.41.kp_ref, ...), custom_call_target="tpu_custom_call", output_to_operand_aliasing={{1}: (6, {})} | custom-call | flops 169869312 | bytes 1000000 | tf_op jit(solution)/shard_map/pallas_call | solution.py:736
Async XLA Ops:
  2.2 5.7 %collective-permute-start = (bf16[288,128]{1,0:T(8,128)(2,1)S(1)}, bf16[288,128]{1,0:T(8,128)(2,1)S(1)}, u32[]{:S(2)}, u32[]{:S(2)}) collective-permute-start(bf16[288,128]{1,0:T(8,128)(2,1)S(1)} %get-tuple-element.57), channel_id=1, source_target_pairs={{0,1},{4,5},{8,9},{12,13},{16,17},{20,21},{24,25},{28,29},{2,6},{1... | collective-permute-start | bytes 221192 | tf_op jit(solution)/shard_map/ppermute | solution.py:27
  5.2 2.6 %collective-permute-start.1 = (bf16[288,128]{1,0:T(8,128)(2,1)S(1)}, bf16[288,128]{1,0:T(8,128)(2,1)S(1)}, u32[]{:S(2)}, u32[]{:S(2)}) collective-permute-start(bf16[288,128]{1,0:T(8,128)(2,1)S(1)} %get-tuple-element.58), channel_id=1, source_target_pairs={{1,2},{5,6},{9,10},{13,14},{17,18},{21,22},{25,26},{29,30},{0,4},{... | collective-permute-start | bytes 221192 | tf_op jit(solution)/shard_map/ppermute | solution.py:27
  5.2 2.7 %collective-permute-start.2 = (bf16[288,128]{1,0:T(8,128)(2,1)S(1)}, bf16[288,128]{1,0:T(8,128)(2,1)S(1)}, u32[]{:S(2)}, u32[]{:S(2)}) collective-permute-start(bf16[288,128]{1,0:T(8,128)(2,1)S(1)} %get-tuple-element.59), channel_id=1, source_target_pairs={{2,3},{6,7},{10,11},{14,15},{18,19},{22,23},{26,27},{30,31},{0,4},... | collective-permute-start | bytes 221192 | tf_op jit(solution)/shard_map/ppermute | solution.py:27
  8.2 4.5 %collective-permute-start.3 = (bf16[336,128]{1,0:T(8,128)(2,1)S(1)}, bf16[336,128]{1,0:T(8,128)(2,1)S(1)}, u32[]{:S(2)}, u32[]{:S(2)}) collective-permute-start(bf16[336,128]{1,0:T(8,128)(2,1)S(1)} %get-tuple-element.70), channel_id=1, source_target_pairs={{4,8},{5,9},{6,10},{7,11},{12,16},{13,17},{14,18},{15,19},{20,24},... | collective-permute-start | bytes 258056 | tf_op jit(solution)/shard_map/ppermute | solution.py:27
  10.1 2.6 %collective-permute-start.4 = (bf16[336,128]{1,0:T(8,128)(2,1)S(1)}, bf16[336,128]{1,0:T(8,128)(2,1)S(1)}, u32[]{:S(2)}, u32[]{:S(2)}) collective-permute-start(bf16[336,128]{1,0:T(8,128)(2,1)S(1)} %get-tuple-element.71), channel_id=1, source_target_pairs={{0,4},{1,5},{2,6},{3,7},{8,12},{9,13},{10,14},{11,15},{16,20},{17,... | collective-permute-start | bytes 258056 | tf_op jit(solution)/shard_map/ppermute | solution.py:27

commit v7 on v5

--- a/solution.py
+++ b/solution.py
@@ -210,7 +210,7 @@
 ):
     cells = wx * wy
     pairs = [
-        (parts_hbm, parts_ref), (f_hbm, f_ref), (st_hbm, st_ref), (t_hbm, t_ref), (dir_hbm, dir_ref),
+        (t_hbm, t_ref), (parts_hbm, parts_ref), (f_hbm, f_ref), (st_hbm, st_ref), (dir_hbm, dir_ref),
         (cls_hbm, cls_ref), (visc_hbm, levels), (diag_hbm, diag_ref),
     ]
     copies = [pltpu.make_async_copy(a, b, sems.at[i]) for i, (a, b) in enumerate(pairs)]
@@ -218,11 +218,11 @@
         copy.start()
     diagonal = lax.broadcasted_iota(jnp.int32, (288, 288), 0) == lax.broadcasted_iota(jnp.int32, (288, 288), 1)
     diagonal = jnp.where(diagonal, F32(penalty), F32(0.0))
-    copies[0].wait()
+    copies[1].wait()
     own = tall([vertex_part(diagonal, parts_ref), diagonal[144:192]])
-    copies[1].wait()
+    copies[2].wait()
     left = tall([vertex_part(f_ref[...], parts_ref).astype(BF), f_ref[pl.ds(144, 48), :]])
-    for copy in copies[2:5]:
+    for copy in (copies[3], copies[4], copies[0]):
         copy.wait()
     short = (turned_dot(left, st_ref[...]) + own).astype(BF)
     z = t_ref.shape[2]

time: 14.2 us -> 14.2 us (level)
  no operation moved by 1% of the time
where the time goes in v7:
time: 14.2 us; the launch traced here: 14 us
  Pallas kernels  6.29 us (44%)
  starting transfers between devices  5.75 us (40%)
  waiting for transfers between devices  1.9 us (13%)
    pallas_call x5, Pallas kernels, call(): pl.pallas_call(body, **keywords, in_specs=[pl.BlockSpec(memory_space=pltp...  6.29 us
    ppermute x5, starting transfers between devices, swap(): lax.ppermute(value, ('gx', 'gy'), pairs + [(high, low) for low, high in p...  5.75 us
    ppermute x5, waiting for transfers between devices, swap(): lax.ppermute(value, ('gx', 'gy'), pairs + [(high, low) for low, high in p...  1.9 us
  transfers between devices with their start and end apart: 5, of which 1 were waited for; matrix products, arithmetic and copies ran while one was open for 0% of the time, Pallas kernels for 17%

profile of v7, /device:TPU:0, one launch (start us, length us, event | category | flops | bytes accessed | tf_op | source)
XLA Modules:
  0.0 14.0 jit_solution(16658557969962878079)
XLA Ops:
  0.0 2.2 %shard_map.82 = (bf16[4,16,48,128]{3,2,1,0:T(8,128)(2,1)S(1)}, f32[3,768,128]{2,1,0:T(8,128)S(1)}, f32[6,16,128]{2,1,0:T(8,128)S(1)}, f32[4,128]{1,0:T(4,128)S(1...) custom-call(f32[4]{0:T(128)} %visc_hbm.1, ...), custom_call_target="tpu_custom_call" | custom-call | flops 113246208 | bytes 1000000 | tf_op jit(solution)/shard_map/pallas_call | solution.py:720
  2.2 3.1 %collective-permute-start = (bf16[288,128]{1,0:T(8,128)(2,1)S(1)}, bf16[288,128]{1,0:T(8,128)(2,1)S(1)}, u32[]{:S(2)}, u32[]{:S(2)}) collective-permute-start(bf16[288,128]{1,0:T(8,128)(2,1)S(1)} %get-tuple-element.55), channel_id=1, source_target_pairs={{0,1},{4,5},{8,9},{12,13},{16,17},{20,21},{24,25},{28,29},{2,6},{1... | collective-permute-start | bytes 221192 | tf_op jit(solution)/shard_map/ppermute | solution.py:27
  5.3 0.0 collective-permute-start.1
  5.3 0.5 %collective-permute-start.2 = (bf16[288,128]{1,0:T(8,128)(2,1)S(1)}, bf16[288,128]{1,0:T(8,128)(2,1)S(1)}, u32[]{:S(2)}, u32[]{:S(2)}) collective-permute-start(bf16[288,128]{1,0:T(8,128)(2,1)S(1)} %get-tuple-element.57), channel_id=1, source_target_pairs={{2,3},{6,7},{10,11},{14,15},{18,19},{22,23},{26,27},{30,31},{0,4},... | collective-permute-start | bytes 221192 | tf_op jit(solution)/shard_map/ppermute | solution.py:27
  5.8 1.9 %shard_map.83 = (f32[6,16,48,128]{3,2,1,0:T(8,128)S(1)}, f32[2,5,8,128]{3,2,1,0:T(8,128)S(1)}, f32[2,16,128]{2,1,0:T(8,128)S(1)}, bf16[384,48]{1,0:T(8,128)(2,1)...) custom-call(bf16[4,16,48,128]{3,2,1,0:T(8,128)(2,1)S(1)} %get-tuple-element.39.l_ref, ...), custom_call_target="tpu_custom_call" | custom-call | flops 452984832 | bytes 1000000 | tf_op jit(solution)/shard_map/pallas_call | solution.py:720
  7.7 0.0 collective-permute-done.swap0_in
  7.7 0.0 collective-permute-done.1.swap1_in
  7.7 0.0 collective-permute-done.2.swap2_in
  7.7 0.3 %shard_map.84 = (f32[2,2,8,128]{3,2,1,0:T(8,128)S(1)}, f32[2,2,8,128]{3,2,1,0:T(8,128)S(1)}, f32[6,16,128]{2,1,0:T(8,128)S(1)}, bf16[288,128]{1,0:T(8,128)(2,1)S...) custom-call(f32[4,128]{1,0:T(4,128)S(1)} %get-tuple-element.38.visc_ref, ...), custom_call_target="tpu_custom_call" | custom-call | flops 56623104 | bytes 1000000 | tf_op jit(solution)/shard_map/pallas_call | solution.py:720
  8.0 2.2 %collective-permute-start.3 = (bf16[336,128]{1,0:T(8,128)(2,1)S(1)}, bf16[336,128]{1,0:T(8,128)(2,1)S(1)}, u32[]{:S(2)}, u32[]{:S(2)}) collective-permute-start(bf16[336,128]{1,0:T(8,128)(2,1)S(1)} %get-tuple-element.68), channel_id=1, source_target_pairs={{4,8},{5,9},{6,10},{7,11},{12,16},{13,17},{14,18},{15,19},{20,24},... | collective-permute-start | bytes 258056 | tf_op jit(solution)/shard_map/ppermute | solution.py:27
  10.2 0.0 collective-permute-start.4
  10.2 0.6 %shard_map.85 = (f32[3,768,128]{2,1,0:T(8,128)S(1)}, f32[4,4,48,128]{3,2,1,0:T(8,128)S(1)}, f32[5,24,128]{2,1,0:T(8,128)S(1)}, f32[4,24,128]{2,1,0:T(8,128)S(1)}, f32[144,768]{1,0:T(8,128)S(1)}) custom-call(f32[4,128]{1,0:T(4,128)S(1)} %get-tuple-element.38.visc_ref, bf16[4,16,48,128]{3,2,1,0:T(8,128)(2,1)S(1)} %get-tuple-element.39.l_ref, ...), custom_call_target="tpu_custom_call" | custom-call | flops 113246208 | bytes 1000000 | tf_op jit(solution)/shard_map/pallas_call | solution.py:720
  10.7 1.9 %collective-permute-done.3.outer_in = bf16[336,128]{1,0:T(8,128)(2,1)S(1)} collective-permute-done((bf16[336,128]{1,0:T(8,128)(2,1)S(1)}, bf16[336,128]{1,0:T(8,128)(2,1)S(1)}, u32[]{:S(2)}, u32[]{:S(2)}) %collective-permute-start.3) | collective-permute-done | bytes 86048 | tf_op jit(solution)/shard_map/ppermute | solution.py:27
  12.6 0.0 collective-permute-done.4.inner_in
  12.6 1.4 %shard_map.86 = (bf16[3,768,128]{2,1,0:T(8,128)(2,1)}, f32[3,768,128]{2,1,0:T(8,128)S(1)}) custom-call(f32[4,128]{1,0:T(4,128)S(1)} %get-tuple-element.38.visc_ref, bf16[4,16,48,128]{3,2,1,0:T(8,128)(2,1)S(1)} %get-tuple-element.39.l_ref, f32[6,16,128]{2,1,0:T(8,128)S(1)} %get-tuple-element.40.kp_ref, ...), custom_call_target="tpu_custom_call", output_to_operand_aliasing={{1}: (6, {})} | custom-call | flops 169869312 | bytes 1000000 | tf_op jit(solution)/shard_map/pallas_call | solution.py:720
Async XLA Ops:
  2.2 5.5 %collective-permute-start = (bf16[288,128]{1,0:T(8,128)(2,1)S(1)}, bf16[288,128]{1,0:T(8,128)(2,1)S(1)}, u32[]{:S(2)}, u32[]{:S(2)}) collective-permute-start(bf16[288,128]{1,0:T(8,128)(2,1)S(1)} %get-tuple-element.55), channel_id=1, source_target_pairs={{0,1},{4,5},{8,9},{12,13},{16,17},{20,21},{24,25},{28,29},{2,6},{1... | collective-permute-start | bytes 221192 | tf_op jit(solution)/shard_map/ppermute | solution.py:27
  5.3 2.4 %collective-permute-start.1 = (bf16[288,128]{1,0:T(8,128)(2,1)S(1)}, bf16[288,128]{1,0:T(8,128)(2,1)S(1)}, u32[]{:S(2)}, u32[]{:S(2)}) collective-permute-start(bf16[288,128]{1,0:T(8,128)(2,1)S(1)} %get-tuple-element.56), channel_id=1, source_target_pairs={{1,2},{5,6},{9,10},{13,14},{17,18},{21,22},{25,26},{29,30},{0,4},{... | collective-permute-start | bytes 221192 | tf_op jit(solution)/shard_map/ppermute | solution.py:27
  5.3 2.4 %collective-permute-start.2 = (bf16[288,128]{1,0:T(8,128)(2,1)S(1)}, bf16[288,128]{1,0:T(8,128)(2,1)S(1)}, u32[]{:S(2)}, u32[]{:S(2)}) collective-permute-start(bf16[288,128]{1,0:T(8,128)(2,1)S(1)} %get-tuple-element.57), channel_id=1, source_target_pairs={{2,3},{6,7},{10,11},{14,15},{18,19},{22,23},{26,27},{30,31},{0,4},... | collective-permute-start | bytes 221192 | tf_op jit(solution)/shard_map/ppermute | solution.py:27
  8.0 4.6 %collective-permute-start.3 = (bf16[336,128]{1,0:T(8,128)(2,1)S(1)}, bf16[336,128]{1,0:T(8,128)(2,1)S(1)}, u32[]{:S(2)}, u32[]{:S(2)}) collective-permute-start(bf16[336,128]{1,0:T(8,128)(2,1)S(1)} %get-tuple-element.68), channel_id=1, source_target_pairs={{4,8},{5,9},{6,10},{7,11},{12,16},{13,17},{14,18},{15,19},{20,24},... | collective-permute-start | bytes 258056 | tf_op jit(solution)/shard_map/ppermute | solution.py:27
  10.2 2.5 %collective-permute-start.4 = (bf16[336,128]{1,0:T(8,128)(2,1)S(1)}, bf16[336,128]{1,0:T(8,128)(2,1)S(1)}, u32[]{:S(2)}, u32[]{:S(2)}) collective-permute-start(bf16[336,128]{1,0:T(8,128)(2,1)S(1)} %get-tuple-element.69), channel_id=1, source_target_pairs={{0,4},{1,5},{2,6},{3,7},{8,12},{9,13},{10,14},{11,15},{16,20},{17,... | collective-permute-start | bytes 258056 | tf_op jit(solution)/shard_map/ppermute | solution.py:27

commit v8 on v5

--- a/solution.py
+++ b/solution.py
@@ -500,7 +500,9 @@
     down_ref[pl.ds(48 * (wy + 1), 48), :] = yd_ref[pl.ds(48 * wx, 48), :]
     diag = diag_ref[pl.ds(0, wy), :]
     high = diag.astype(BF).astype(F32)
-    rim = [plane(0, 0, 0), high, edge_high[0:1], diag - high, edge_low[0:1]]
+    first = plane(0, 0, 0)
+    rim = [first[4 * y : 4 * y + 3] for y in range(wy + 1)]
+    rim += [high, edge_high[0:1], diag - high, edge_low[0:1]]
     rim += [misc_u[wx : wx + 1], kp_ref[0, 0:wy], misc_d[wx : wx + 1]]
     put_tail(down_ref, 48 * (wy + 2), rim)
     corner = (wx - 1) * wy
@@ -605,11 +607,15 @@
     row = lambda i, col: kp_ref[i, pl.ds(col, 1), :]
     traces = [from_high(48 * j, 48) for j in range(wy + 2)]
     delta = dot(mx_ref[pl.ds(288, 96), :], wide(traces))
-    rim_x = from_high(48 * (wy + 2), tail_rows(rows + 3 * wy + 4)).astype(F32)
+    rim_x = from_high(48 * (wy + 2), tail_rows(6 * wy + 7)).astype(F32)
+    gap = jnp.zeros((1, z), F32)
+    ahead = [part for j in range(wy + 1) for part in (rim_x[3 * j : 3 * j + 3], gap)]
+    ahead = tall(ahead + [jnp.zeros((rows - 4 * (wy + 1), z), F32)])
+    rim_x = rim_x[3 * (wy + 1) :]
     rim_l = from_low(48 * wy, tail_rows(rows + 32 + 3 * (wy + 2) - 1)).astype(F32)
     misc_d = read_tail(yd_ref, wx, 0)[2]
     misc_u = read_tail(yu_ref, wx, 1)[2]
-    flags_high = rim_x[rows + 2 * (wy + 1) : rows + 3 * wy + 4]
+    flags_high = rim_x[2 * (wy + 1) : 3 * wy + 4]
     corner = (wx - 1) * wy
     arrived = [from_low(48 * y, 48) for y in range(wy)]
     arrived_corners = slot_corners(arrived, parts_ref, 1)
@@ -662,11 +668,11 @@
             one = rim_l[at : at + 16] * flag
             lines[2].append(corners + one[0:8] + z_prev(one[8:16]))
     low, before, first = [merge(part[1::2], part[0::2]) for part in lines]
-    top = v_ref[wx] + before + rim_x[0:rows]
+    top = v_ref[wx] + before + ahead
     values = [(v_ref[0] + first + rim_l[0:rows]) * inv_ref[0]]
     values += [v_ref[i] * inv_ref[i] for i in range(1, wx - 1)]
     values += [(v_ref[wx - 1] + low) * inv_ref[wx - 1]]
-    diag = rim_x[rows : rows + wy + 1] + rim_x[rows + wy + 1 : rows + 2 * (wy + 1)]
+    diag = rim_x[0 : wy + 1] + rim_x[wy + 1 : 2 * (wy + 1)]
     parts = [jnp.broadcast_to(diag[j : j + 1], (4, z)) for j in range(wy + 1)]
     values += [top * reciprocal(tall(parts + [jnp.zeros((rows - 4 * (wy + 1), z), F32)]))]
     high = [pltpu.roll(value, rows - 4, 0) for value in values]
@@ -737,7 +743,7 @@
     vm = pltpu.VMEM
     bind = lambda body: functools.partial(body, wx, wy)
     y_message = vm((48 * wx + 48 + tail_rows(8 * ((wx + 2) // 2) + 8 + 3 * wx + 4), z), BF)
-    x_message = vm((48 * (wy + 2) + tail_rows(rows + 3 * wy + 4), z), BF)
+    x_message = vm((48 * (wy + 2) + tail_rows(6 * wy + 7), z), BF)
 
     (lifted, nat, flags, visc, diag, s_turned, f_map, parts, va, v1a, v3, *swaps) = call(
         bind(first_kernel),

time: 14.2 us -> 14.1 us (level)
  transfers between devices with their start and end apart: 5 -> 5, of which waited for: 1 -> 1; matrix products, arithmetic and copies ran while one was open for 0% -> 0% of each run, Pallas kernels for 17% -> 18%
where the time goes in v8:
time: 14.1 us; the launch traced here: 13.9 us
  Pallas kernels  6.27 us (44%)
  starting transfers between devices  5.74 us (41%)
  waiting for transfers between devices  1.86 us (13%)
    pallas_call x5, Pallas kernels, call(): pl.pallas_call(body, **keywords, in_specs=[pl.BlockSpec(memory_space=pltp...  6.27 us
    ppermute x5, starting transfers between devices, swap(): lax.ppermute(value, ('gx', 'gy'), pairs + [(high, low) for low, high in p...  5.74 us
    ppermute x5, waiting for transfers between devices, swap(): lax.ppermute(value, ('gx', 'gy'), pairs + [(high, low) for low, high in p...  1.86 us
  transfers between devices with their start and end apart: 5, of which 1 were waited for; matrix products, arithmetic and copies ran while one was open for 0% of the time, Pallas kernels for 18%

profile of v8, /device:TPU:0, one launch (start us, length us, event | category | flops | bytes accessed | tf_op | source)
XLA Modules:
  0.0 13.9 jit_solution(11998708686416347515)
XLA Ops:
  0.0 2.2 %shard_map.82 = (bf16[4,16,48,128]{3,2,1,0:T(8,128)(2,1)S(1)}, f32[3,768,128]{2,1,0:T(8,128)S(1)}, f32[6,16,128]{2,1,0:T(8,128)S(1)}, f32[4,128]{1,0:T(4,128)S(1...) custom-call(f32[4]{0:T(128)} %visc_hbm.1, ...), custom_call_target="tpu_custom_call" | custom-call | flops 113246208 | bytes 1000000 | tf_op jit(solution)/shard_map/pallas_call | solution.py:726
  2.2 3.1 %collective-permute-start = (bf16[288,128]{1,0:T(8,128)(2,1)S(1)}, bf16[288,128]{1,0:T(8,128)(2,1)S(1)}, u32[]{:S(2)}, u32[]{:S(2)}) collective-permute-start(bf16[288,128]{1,0:T(8,128)(2,1)S(1)} %get-tuple-element.55), channel_id=1, source_target_pairs={{0,1},{4,5},{8,9},{12,13},{16,17},{20,21},{24,25},{28,29},{2,6},{1... | collective-permute-start | bytes 221192 | tf_op jit(solution)/shard_map/ppermute | solution.py:27
  5.3 0.0 collective-permute-start.1
  5.3 0.5 %collective-permute-start.2 = (bf16[288,128]{1,0:T(8,128)(2,1)S(1)}, bf16[288,128]{1,0:T(8,128)(2,1)S(1)}, u32[]{:S(2)}, u32[]{:S(2)}) collective-permute-start(bf16[288,128]{1,0:T(8,128)(2,1)S(1)} %get-tuple-element.57), channel_id=1, source_target_pairs={{2,3},{6,7},{10,11},{14,15},{18,19},{22,23},{26,27},{30,31},{0,4},... | collective-permute-start | bytes 221192 | tf_op jit(solution)/shard_map/ppermute | solution.py:27
  5.8 1.9 %shard_map.83 = (f32[6,16,48,128]{3,2,1,0:T(8,128)S(1)}, f32[2,5,8,128]{3,2,1,0:T(8,128)S(1)}, f32[2,16,128]{2,1,0:T(8,128)S(1)}, bf16[384,48]{1,0:T(8,128)(2,1)...) custom-call(bf16[4,16,48,128]{3,2,1,0:T(8,128)(2,1)S(1)} %get-tuple-element.39.l_ref, ...), custom_call_target="tpu_custom_call" | custom-call | flops 452984832 | bytes 1000000 | tf_op jit(solution)/shard_map/pallas_call | solution.py:726
  7.6 0.0 collective-permute-done.swap0_in
  7.6 0.0 collective-permute-done.1.swap1_in
  7.7 0.0 collective-permute-done.2.swap2_in
  7.7 0.3 %shard_map.84 = (f32[2,2,8,128]{3,2,1,0:T(8,128)S(1)}, f32[2,2,8,128]{3,2,1,0:T(8,128)S(1)}, f32[6,16,128]{2,1,0:T(8,128)S(1)}, bf16[288,128]{1,0:T(8,128)(2,1)S...) custom-call(f32[4,128]{1,0:T(4,128)S(1)} %get-tuple-element.38.visc_ref, ...), custom_call_target="tpu_custom_call" | custom-call | flops 56623104 | bytes 1000000 | tf_op jit(solution)/shard_map/pallas_call | solution.py:726
  8.0 2.1 %collective-permute-start.3 = (bf16[320,128]{1,0:T(8,128)(2,1)S(1)}, bf16[320,128]{1,0:T(8,128)(2,1)S(1)}, u32[]{:S(2)}, u32[]{:S(2)}) collective-permute-start(bf16[320,128]{1,0:T(8,128)(2,1)S(1)} %get-tuple-element.68), channel_id=1, source_target_pairs={{4,8},{5,9},{6,10},{7,11},{12,16},{13,17},{14,18},{15,19},{20,24},... | collective-permute-start | bytes 245768 | tf_op jit(solution)/shard_map/ppermute | solution.py:27
  10.1 0.0 collective-permute-start.4
  10.1 0.6 %shard_map.85 = (f32[3,768,128]{2,1,0:T(8,128)S(1)}, f32[4,4,48,128]{3,2,1,0:T(8,128)S(1)}, f32[5,24,128]{2,1,0:T(8,128)S(1)}, f32[4,24,128]{2,1,0:T(8,128)S(1)}, f32[144,768]{1,0:T(8,128)S(1)}) custom-call(f32[4,128]{1,0:T(4,128)S(1)} %get-tuple-element.38.visc_ref, bf16[4,16,48,128]{3,2,1,0:T(8,128)(2,1)S(1)} %get-tuple-element.39.l_ref, ...), custom_call_target="tpu_custom_call" | custom-call | flops 113246208 | bytes 1000000 | tf_op jit(solution)/shard_map/pallas_call | solution.py:726
  10.7 1.8 %collective-permute-done.3.outer_in = bf16[320,128]{1,0:T(8,128)(2,1)S(1)} collective-permute-done((bf16[320,128]{1,0:T(8,128)(2,1)S(1)}, bf16[320,128]{1,0:T(8,128)(2,1)S(1)}, u32[]{:S(2)}, u32[]{:S(2)}) %collective-permute-start.3) | collective-permute-done | bytes 81952 | tf_op jit(solution)/shard_map/ppermute | solution.py:27
  12.6 0.0 collective-permute-done.4.inner_in
  12.6 1.4 %shard_map.86 = (bf16[3,768,128]{2,1,0:T(8,128)(2,1)}, f32[3,768,128]{2,1,0:T(8,128)S(1)}) custom-call(f32[4,128]{1,0:T(4,128)S(1)} %get-tuple-element.38.visc_ref, bf16[4,16,48,128]{3,2,1,0:T(8,128)(2,1)S(1)} %get-tuple-element.39.l_ref, f32[6,16,128]{2,1,0:T(8,128)S(1)} %get-tuple-element.40.kp_ref, ...), custom_call_target="tpu_custom_call", output_to_operand_aliasing={{1}: (6, {})} | custom-call | flops 169869312 | bytes 1000000 | tf_op jit(solution)/shard_map/pallas_call | solution.py:726
Async XLA Ops:
  2.2 5.5 %collective-permute-start = (bf16[288,128]{1,0:T(8,128)(2,1)S(1)}, bf16[288,128]{1,0:T(8,128)(2,1)S(1)}, u32[]{:S(2)}, u32[]{:S(2)}) collective-permute-start(bf16[288,128]{1,0:T(8,128)(2,1)S(1)} %get-tuple-element.55), channel_id=1, source_target_pairs={{0,1},{4,5},{8,9},{12,13},{16,17},{20,21},{24,25},{28,29},{2,6},{1... | collective-permute-start | bytes 221192 | tf_op jit(solution)/shard_map/ppermute | solution.py:27
  5.3 2.4 %collective-permute-start.1 = (bf16[288,128]{1,0:T(8,128)(2,1)S(1)}, bf16[288,128]{1,0:T(8,128)(2,1)S(1)}, u32[]{:S(2)}, u32[]{:S(2)}) collective-permute-start(bf16[288,128]{1,0:T(8,128)(2,1)S(1)} %get-tuple-element.56), channel_id=1, source_target_pairs={{1,2},{5,6},{9,10},{13,14},{17,18},{21,22},{25,26},{29,30},{0,4},{... | collective-permute-start | bytes 221192 | tf_op jit(solution)/shard_map/ppermute | solution.py:27
  5.3 2.4 %collective-permute-start.2 = (bf16[288,128]{1,0:T(8,128)(2,1)S(1)}, bf16[288,128]{1,0:T(8,128)(2,1)S(1)}, u32[]{:S(2)}, u32[]{:S(2)}) collective-permute-start(bf16[288,128]{1,0:T(8,128)(2,1)S(1)} %get-tuple-element.57), channel_id=1, source_target_pairs={{2,3},{6,7},{10,11},{14,15},{18,19},{22,23},{26,27},{30,31},{0,4},... | collective-permute-start | bytes 221192 | tf_op jit(solution)/shard_map/ppermute | solution.py:27
  8.0 4.6 %collective-permute-start.3 = (bf16[320,128]{1,0:T(8,128)(2,1)S(1)}, bf16[320,128]{1,0:T(8,128)(2,1)S(1)}, u32[]{:S(2)}, u32[]{:S(2)}) collective-permute-start(bf16[320,128]{1,0:T(8,128)(2,1)S(1)} %get-tuple-element.68), channel_id=1, source_target_pairs={{4,8},{5,9},{6,10},{7,11},{12,16},{13,17},{14,18},{15,19},{20,24},... | collective-permute-start | bytes 245768 | tf_op jit(solution)/shard_map/ppermute | solution.py:27
  10.1 2.4 %collective-permute-start.4 = (bf16[320,128]{1,0:T(8,128)(2,1)S(1)}, bf16[320,128]{1,0:T(8,128)(2,1)S(1)}, u32[]{:S(2)}, u32[]{:S(2)}) collective-permute-start(bf16[320,128]{1,0:T(8,128)(2,1)S(1)} %get-tuple-element.69), channel_id=1, source_target_pairs={{0,4},{1,5},{2,6},{3,7},{8,12},{9,13},{10,14},{11,15},{16,20},{17,... | collective-permute-start | bytes 245768 | tf_op jit(solution)/shard_map/ppermute | solution.py:27

commit v9 on v8

--- a/solution.py
+++ b/solution.py
@@ -710,8 +710,10 @@
                 for b, value in enumerate(between(lines[0][a], lines[1][a])):
                     at = pl.ds(cells * (16 * c + 4 * a + b), cells)
                     held[d, at, :] = (r_ref[d, at, :] + value).astype(BF)
-        copies.append(pltpu.make_async_copy(held.at[d], out_hbm.at[d], sems.at[d]))
-        copies[d].start()
+        if d:
+            part = pl.ds(0, 2) if d == 1 else pl.ds(2, 1)
+            copies.append(pltpu.make_async_copy(held.at[part], out_hbm.at[part], sems.at[d - 1]))
+            copies[-1].start()
     for copy in copies:
         copy.wait()
 
@@ -804,7 +806,7 @@
             visc, lifted, flags, parts, mx, ownx, residual, late, vs, inverse, v1, yd, yu, outer, inner,
         ),
         (jax.ShapeDtypeStruct((3, 48 * cells, z), BF), vm((3, 48 * cells, z), F32)),
-        [vm((3, 48 * cells, z), BF), vm((2, 4 * wy * (wx + 1), z), F32), pltpu.SemaphoreType.DMA((3,))], 6 * per_hex,
+        [vm((3, 48 * cells, z), BF), vm((2, 4 * wy * (wx + 1), z), F32), pltpu.SemaphoreType.DMA((2,))], 6 * per_hex,
         aliases={6: 1},
     )
     return out.reshape(traces.shape)

time: 14.1 us -> 14.1 us (level)
  no operation moved by 1% of the time
where the time goes in v9:
time: 14.1 us; the launch traced here: 13.9 us
  Pallas kernels  6.28 us (45%)
  starting transfers between devices  5.74 us (41%)
  waiting for transfers between devices  1.86 us (13%)
    pallas_call x5, Pallas kernels, call(): pl.pallas_call(body, **keywords, in_specs=[pl.BlockSpec(memory_space=pltp...  6.28 us
    ppermute x5, starting transfers between devices, swap(): lax.ppermute(value, ('gx', 'gy'), pairs + [(high, low) for low, high in p...  5.74 us
    ppermute x5, waiting for transfers between devices, swap(): lax.ppermute(value, ('gx', 'gy'), pairs + [(high, low) for low, high in p...  1.86 us
  transfers between devices with their start and end apart: 5, of which 1 were waited for; matrix products, arithmetic and copies ran while one was open for 0% of the time, Pallas kernels for 18%

profile of v9, /device:TPU:0, one launch (start us, length us, event | category | flops | bytes accessed | tf_op | source)
XLA Modules:
  0.0 13.9 jit_solution(7330280011780043072)
XLA Ops:
  0.0 2.2 %shard_map.82 = (bf16[4,16,48,128]{3,2,1,0:T(8,128)(2,1)S(1)}, f32[3,768,128]{2,1,0:T(8,128)S(1)}, f32[6,16,128]{2,1,0:T(8,128)S(1)}, f32[4,128]{1,0:T(4,128)S(1...) custom-call(f32[4]{0:T(128)} %visc_hbm.1, ...), custom_call_target="tpu_custom_call" | custom-call | flops 113246208 | bytes 1000000 | tf_op jit(solution)/shard_map/pallas_call | solution.py:728
  2.2 3.1 %collective-permute-start = (bf16[288,128]{1,0:T(8,128)(2,1)S(1)}, bf16[288,128]{1,0:T(8,128)(2,1)S(1)}, u32[]{:S(2)}, u32[]{:S(2)}) collective-permute-start(bf16[288,128]{1,0:T(8,128)(2,1)S(1)} %get-tuple-element.55), channel_id=1, source_target_pairs={{0,1},{4,5},{8,9},{12,13},{16,17},{20,21},{24,25},{28,29},{2,6},{1... | collective-permute-start | bytes 221192 | tf_op jit(solution)/shard_map/ppermute | solution.py:27
  5.3 0.0 collective-permute-start.1
  5.3 0.5 %collective-permute-start.2 = (bf16[288,128]{1,0:T(8,128)(2,1)S(1)}, bf16[288,128]{1,0:T(8,128)(2,1)S(1)}, u32[]{:S(2)}, u32[]{:S(2)}) collective-permute-start(bf16[288,128]{1,0:T(8,128)(2,1)S(1)} %get-tuple-element.57), channel_id=1, source_target_pairs={{2,3},{6,7},{10,11},{14,15},{18,19},{22,23},{26,27},{30,31},{0,4},... | collective-permute-start | bytes 221192 | tf_op jit(solution)/shard_map/ppermute | solution.py:27
  5.8 1.9 %shard_map.83 = (f32[6,16,48,128]{3,2,1,0:T(8,128)S(1)}, f32[2,5,8,128]{3,2,1,0:T(8,128)S(1)}, f32[2,16,128]{2,1,0:T(8,128)S(1)}, bf16[384,48]{1,0:T(8,128)(2,1)...) custom-call(bf16[4,16,48,128]{3,2,1,0:T(8,128)(2,1)S(1)} %get-tuple-element.39.l_ref, ...), custom_call_target="tpu_custom_call" | custom-call | flops 452984832 | bytes 1000000 | tf_op jit(solution)/shard_map/pallas_call | solution.py:728
  7.6 0.0 collective-permute-done.swap0_in
  7.6 0.0 collective-permute-done.1.swap1_in
  7.7 0.0 collective-permute-done.2.swap2_in
  7.7 0.3 %shard_map.84 = (f32[2,2,8,128]{3,2,1,0:T(8,128)S(1)}, f32[2,2,8,128]{3,2,1,0:T(8,128)S(1)}, f32[6,16,128]{2,1,0:T(8,128)S(1)}, bf16[288,128]{1,0:T(8,128)(2,1)S...) custom-call(f32[4,128]{1,0:T(4,128)S(1)} %get-tuple-element.38.visc_ref, ...), custom_call_target="tpu_custom_call" | custom-call | flops 56623104 | bytes 1000000 | tf_op jit(solution)/shard_map/pallas_call | solution.py:728
  8.0 2.1 %collective-permute-start.3 = (bf16[320,128]{1,0:T(8,128)(2,1)S(1)}, bf16[320,128]{1,0:T(8,128)(2,1)S(1)}, u32[]{:S(2)}, u32[]{:S(2)}) collective-permute-start(bf16[320,128]{1,0:T(8,128)(2,1)S(1)} %get-tuple-element.68), channel_id=1, source_target_pairs={{4,8},{5,9},{6,10},{7,11},{12,16},{13,17},{14,18},{15,19},{20,24},... | collective-permute-start | bytes 245768 | tf_op jit(solution)/shard_map/ppermute | solution.py:27
  10.1 0.0 collective-permute-start.4
  10.1 0.6 %shard_map.85 = (f32[3,768,128]{2,1,0:T(8,128)S(1)}, f32[4,4,48,128]{3,2,1,0:T(8,128)S(1)}, f32[5,24,128]{2,1,0:T(8,128)S(1)}, f32[4,24,128]{2,1,0:T(8,128)S(1)}, f32[144,768]{1,0:T(8,128)S(1)}) custom-call(f32[4,128]{1,0:T(4,128)S(1)} %get-tuple-element.38.visc_ref, bf16[4,16,48,128]{3,2,1,0:T(8,128)(2,1)S(1)} %get-tuple-element.39.l_ref, ...), custom_call_target="tpu_custom_call" | custom-call | flops 113246208 | bytes 1000000 | tf_op jit(solution)/shard_map/pallas_call | solution.py:728
  10.7 1.8 %collective-permute-done.3.outer_in = bf16[320,128]{1,0:T(8,128)(2,1)S(1)} collective-permute-done((bf16[320,128]{1,0:T(8,128)(2,1)S(1)}, bf16[320,128]{1,0:T(8,128)(2,1)S(1)}, u32[]{:S(2)}, u32[]{:S(2)}) %collective-permute-start.3) | collective-permute-done | bytes 81952 | tf_op jit(solution)/shard_map/ppermute | solution.py:27
  12.6 0.0 collective-permute-done.4.inner_in
  12.6 1.4 %shard_map.86 = (bf16[3,768,128]{2,1,0:T(8,128)(2,1)}, f32[3,768,128]{2,1,0:T(8,128)S(1)}) custom-call(f32[4,128]{1,0:T(4,128)S(1)} %get-tuple-element.38.visc_ref, bf16[4,16,48,128]{3,2,1,0:T(8,128)(2,1)S(1)} %get-tuple-element.39.l_ref, f32[6,16,128]{2,1,0:T(8,128)S(1)} %get-tuple-element.40.kp_ref, ...), custom_call_target="tpu_custom_call", output_to_operand_aliasing={{1}: (6, {})} | custom-call | flops 169869312 | bytes 1000000 | tf_op jit(solution)/shard_map/pallas_call | solution.py:728
Async XLA Ops:
  2.2 5.5 %collective-permute-start = (bf16[288,128]{1,0:T(8,128)(2,1)S(1)}, bf16[288,128]{1,0:T(8,128)(2,1)S(1)}, u32[]{:S(2)}, u32[]{:S(2)}) collective-permute-start(bf16[288,128]{1,0:T(8,128)(2,1)S(1)} %get-tuple-element.55), channel_id=1, source_target_pairs={{0,1},{4,5},{8,9},{12,13},{16,17},{20,21},{24,25},{28,29},{2,6},{1... | collective-permute-start | bytes 221192 | tf_op jit(solution)/shard_map/ppermute | solution.py:27
  5.3 2.4 %collective-permute-start.1 = (bf16[288,128]{1,0:T(8,128)(2,1)S(1)}, bf16[288,128]{1,0:T(8,128)(2,1)S(1)}, u32[]{:S(2)}, u32[]{:S(2)}) collective-permute-start(bf16[288,128]{1,0:T(8,128)(2,1)S(1)} %get-tuple-element.56), channel_id=1, source_target_pairs={{1,2},{5,6},{9,10},{13,14},{17,18},{21,22},{25,26},{29,30},{0,4},{... | collective-permute-start | bytes 221192 | tf_op jit(solution)/shard_map/ppermute | solution.py:27
  5.3 2.4 %collective-permute-start.2 = (bf16[288,128]{1,0:T(8,128)(2,1)S(1)}, bf16[288,128]{1,0:T(8,128)(2,1)S(1)}, u32[]{:S(2)}, u32[]{:S(2)}) collective-permute-start(bf16[288,128]{1,0:T(8,128)(2,1)S(1)} %get-tuple-element.57), channel_id=1, source_target_pairs={{2,3},{6,7},{10,11},{14,15},{18,19},{22,23},{26,27},{30,31},{0,4},... | collective-permute-start | bytes 221192 | tf_op jit(solution)/shard_map/ppermute | solution.py:27
  8.0 4.6 %collective-permute-start.3 = (bf16[320,128]{1,0:T(8,128)(2,1)S(1)}, bf16[320,128]{1,0:T(8,128)(2,1)S(1)}, u32[]{:S(2)}, u32[]{:S(2)}) collective-permute-start(bf16[320,128]{1,0:T(8,128)(2,1)S(1)} %get-tuple-element.68), channel_id=1, source_target_pairs={{4,8},{5,9},{6,10},{7,11},{12,16},{13,17},{14,18},{15,19},{20,24},... | collective-permute-start | bytes 245768 | tf_op jit(solution)/shard_map/ppermute | solution.py:27
  10.1 2.4 %collective-permute-start.4 = (bf16[320,128]{1,0:T(8,128)(2,1)S(1)}, bf16[320,128]{1,0:T(8,128)(2,1)S(1)}, u32[]{:S(2)}, u32[]{:S(2)}) collective-permute-start(bf16[320,128]{1,0:T(8,128)(2,1)S(1)} %get-tuple-element.69), channel_id=1, source_target_pairs={{0,4},{1,5},{2,6},{3,7},{8,12},{9,13},{10,14},{11,15},{16,20},{17,... | collective-permute-start | bytes 245768 | tf_op jit(solution)/shard_map/ppermute | solution.py:27
